TPU v7x, 256 devices: a whole 4x4x8 slice. The times are simulated.
256 devices in a mesh: sample: 16 (over x_hi, z), atom: 16 (over y, x_lo, core).
Axes of the slice: x: 4 (x_hi: 2, x_lo: 2; x = x_hi * 2 + x_lo), y: 4, z: 8, core: 2. Of those that a mesh axis runs over, the one named last changes fastest.
Arguments:
- atom_state: bfloat16 [16, 16384, 128], P('sample', 'atom'), may hold values from -6 to 6
- norm_gain: float32 [128], replicated, may hold values from 0.25 to 1.75
- query_weight: bfloat16 [128, 128], replicated, may hold values from -0.5 to 0.5
- key_weight: bfloat16 [128, 128], replicated, may hold values from -0.5 to 0.5
- value_weight: bfloat16 [128, 128], replicated, may hold values from -0.5 to 0.5
- out_weight: bfloat16 [128, 128], replicated, may hold values from -0.5 to 0.5
- token_weight: bfloat16 [128, 768], replicated, may hold values from -0.5 to 0.5
- pair_bias: float32 [512, 4, 32, 128], P('atom'), may hold values from -4 to 300
- key_start: int32 [512], P('atom'), may hold values from 0 to 16256, as said below
- atom_token: int32 [16384], replicated, may hold values from 0 to 2047, as said below
- cotangent_state: bfloat16 [16, 16384, 128], P('sample', 'atom'), may hold values from -6 to 6
- cotangent_tokens: bfloat16 [16, 2048, 768], P('sample', 'atom'), may hold values from -6 to 6
Outputs:
- state_out: bfloat16 [16, 16384, 128], P('sample', 'atom')
- token_rows: bfloat16 [16, 2048, 768], P('sample', 'atom')
- grad_state: float32 [16, 16384, 128], P('sample', 'atom')
- grad_gain: float32 [128], replicated
- grad_query: float32 [128, 128], replicated
- grad_key: float32 [128, 128], replicated
- grad_value: float32 [128, 128], replicated
- grad_output: float32 [128, 128], replicated
- grad_token: float32 [128, 768], replicated
Inputs may be any that keep to these rules, and one draw needn't show every extreme that they name: Window w reads key atoms key_start[w] to key_start[w] + 127; key_start[w] - 32 * w lies between 32 // 2 - 128 // 2 - 32 and 32 // 2 - 128 // 2 + 32 except where it is clipped into the grid. `atom_token`: nondecreasing along the atoms; every token has one atom or more; atom 0 belongs to token 0; for 0 < b < 16 the first atom of token b * 128 lies between 128 and 256 atoms after atom b * 1024, and both ends are reached.
All inputs are finite; a program needn't handle non-finite values.
Results may differ from a plain program's by a relative error of at most 0.012.
Values may be sent and summed in bfloat16 or wider, within the bound.
A program may use at most 64 MiB of HBM per device.

v0:
```python
import math

import jax
import jax.numpy as jnp
from jax import lax
from jax.sharding import PartitionSpec as P

norm_eps = 1e-05
highest = lax.Precision.HIGHEST


def extended(cells, sides, width):
    for axis, dim in sides:
        count = lax.axis_size(axis)
        ends = count - 1
        head = lax.slice_in_dim(cells, 0, width, axis=dim)
        tail = lax.slice_in_dim(cells, cells.shape[dim] - width, cells.shape[dim], axis=dim)
        cells = jnp.concatenate(
            [
                lax.ppermute(tail, axis, [(i, (i + 1) % count) for i in range(ends)]),
                cells,
                lax.ppermute(head, axis, [((i + 1) % count, i) for i in range(ends)]),
            ],
            axis=dim,
        )
    return cells


def shifted(value, axis, steps):
    count = lax.axis_size(axis)
    initial, last = (max(0, -steps), min(count, count - steps))
    return lax.ppermute(value, axis, [(source, source + steps) for source in range(initial, last)])


def normalize(state_rows, norm_gain):
    widened = state_rows.astype(jnp.float32)
    average = jnp.mean(widened, axis=-1, keepdims=True)
    centred = widened - average
    variance = jnp.mean(centred * centred, axis=-1, keepdims=True)
    inverse = lax.rsqrt(variance + norm_eps)
    unit_rows = centred * inverse
    return (unit_rows, inverse, (unit_rows * norm_gain).astype(jnp.bfloat16))


def silu_slope(values):
    sigma = jax.nn.sigmoid(values)
    return sigma * (1.0 + values * (1.0 - sigma))


def token_sums(values, slots, valid, slot_count):
    sample_count, row_count, width = values.shape
    block = math.gcd(row_count, 128)
    block_count = row_count // block
    slot_pos = jnp.arange(block, dtype=jnp.int32)
    buffer = jnp.zeros((sample_count, slot_count + 2 * block, width), jnp.float32)

    def add_block(index, acc):
        first_row = index * block
        part_slots = lax.dynamic_slice_in_dim(slots, first_row, block)
        part_valid = lax.dynamic_slice_in_dim(valid, first_row, block)
        start = jnp.clip(part_slots[0], -block, slot_count)
        selector = (
            ((part_slots - start)[:, None] == slot_pos[None, :]) & part_valid[:, None]
        ).astype(jnp.float32)
        rows = lax.dynamic_slice_in_dim(values, first_row, block, 1)
        contrib = jnp.einsum("rk,srw->skw", selector, rows, precision=highest)
        place = start + block
        current = lax.dynamic_slice_in_dim(acc, place, block, 1)
        return lax.dynamic_update_slice_in_dim(acc, current + contrib, place, 1)

    buffer = lax.fori_loop(0, block_count, add_block, buffer)
    return buffer[:, block : block + slot_count]


def on_device(
    atom_state,
    norm_gain,
    query_weight,
    key_weight,
    value_weight,
    out_weight,
    token_weight,
    pair_bias,
    key_start,
    atom_token,
    cotangent_state,
    cotangent_tokens,
):
    sample_count, row_count, channels = atom_state.shape
    window_count, head_count, query_rows, key_count = pair_bias.shape
    head_dim = channels // head_count
    factor = head_dim ** (-0.5)
    token_count = cotangent_tokens.shape[1]
    device_pos = lax.axis_index("atom")
    first_atom = device_pos * row_count
    base_token = device_pos * token_count
    lower_token = base_token - token_count
    unit_rows, inverse, normed = normalize(atom_state, norm_gain)
    pair_weight = jnp.concatenate([key_weight, value_weight], axis=1)
    queries = jnp.dot(normed, query_weight, preferred_element_type=jnp.float32).astype(jnp.bfloat16)
    pair_own = jnp.dot(normed, pair_weight, preferred_element_type=jnp.float32).astype(jnp.bfloat16)
    pair_halo = extended(pair_own, (("atom", 1),), key_count)
    starting = key_start - (first_atom - key_count)
    offsets = starting[:, None] + jnp.arange(key_count, dtype=jnp.int32)[None, :]
    window_pairs = jnp.take(pair_halo, offsets, axis=1)
    key_heads = window_pairs[..., :channels].reshape(
        sample_count, window_count, key_count, head_count, head_dim
    )
    value_heads = window_pairs[..., channels:].reshape(
        sample_count, window_count, key_count, head_count, head_dim
    )
    query_heads = queries.reshape(sample_count, window_count, query_rows, head_count, head_dim)
    scores = (
        jnp.einsum("swqhd,swkhd->swhqk", query_heads, key_heads, preferred_element_type=jnp.float32)
        * factor
        + pair_bias[None]
    )
    softmaxed = jax.nn.softmax(scores, axis=-1)
    softmaxed_low = softmaxed.astype(jnp.bfloat16)
    attended = (
        jnp.einsum(
            "swhqk,swkhd->swqhd", softmaxed_low, value_heads, preferred_element_type=jnp.float32
        )
        .astype(jnp.bfloat16)
        .reshape(sample_count, row_count, channels)
    )
    state_out = (
        atom_state.astype(jnp.float32)
        + jnp.dot(attended, out_weight, preferred_element_type=jnp.float32)
    ).astype(jnp.bfloat16)
    own_tokens = lax.dynamic_slice_in_dim(atom_token, first_atom, row_count)
    local_slot = own_tokens - lower_token
    bounds = jnp.searchsorted(
        atom_token, lower_token + jnp.arange(3 * token_count + 1, dtype=jnp.int32)
    )
    counts = (bounds[1:] - bounds[:-1]).astype(jnp.float32)
    own_counts = counts[token_count : 2 * token_count]
    before = jnp.dot(state_out, token_weight, preferred_element_type=jnp.float32)
    all_valid = jnp.ones((row_count,), jnp.bool_)
    partial_value = token_sums(jax.nn.silu(before), local_slot, all_valid, 2 * token_count)
    from_above = shifted(partial_value[:, :token_count].astype(jnp.bfloat16), "atom", -1).astype(
        jnp.float32
    )
    totals = partial_value[:, token_count:] + from_above
    token_rows = (totals / own_counts[None, :, None]).astype(jnp.bfloat16)
    from_below = shifted(cotangent_tokens, "atom", 1)
    token_back = jnp.concatenate([from_below, cotangent_tokens], axis=1)
    atom_counts = jnp.take(counts, local_slot)
    per_atom = (
        jnp.take(token_back, local_slot, axis=1).astype(jnp.float32) / atom_counts[None, :, None]
    )
    active_back = (per_atom * silu_slope(before)).astype(jnp.bfloat16)
    token_sum = jnp.einsum(
        "src,srt->ct", state_out, active_back, preferred_element_type=jnp.float32
    )
    state_back = (
        cotangent_state.astype(jnp.float32)
        + jnp.dot(active_back, token_weight.T, preferred_element_type=jnp.float32)
    ).astype(jnp.bfloat16)
    output_sum = jnp.einsum("src,srd->cd", attended, state_back, preferred_element_type=jnp.float32)
    attended_back = jnp.dot(state_back, out_weight.T, preferred_element_type=jnp.float32).astype(
        jnp.bfloat16
    )
    heads_back = attended_back.reshape(sample_count, window_count, query_rows, head_count, head_dim)
    softmax_back = jnp.einsum(
        "swqhd,swkhd->swhqk", heads_back, value_heads, preferred_element_type=jnp.float32
    )
    scores_back = softmaxed * (
        softmax_back - jnp.sum(softmaxed * softmax_back, axis=-1, keepdims=True)
    )
    scores_low = scores_back.astype(jnp.bfloat16)
    query_back = (
        jnp.einsum("swhqk,swkhd->swqhd", scores_low, key_heads, preferred_element_type=jnp.float32)
        * factor
    ).reshape(sample_count, row_count, channels)
    keys_back = (
        jnp.einsum(
            "swhqk,swqhd->swkhd", scores_low, query_heads, preferred_element_type=jnp.float32
        )
        * factor
    )
    values_back = jnp.einsum(
        "swhqk,swqhd->swkhd", softmaxed_low, heads_back, preferred_element_type=jnp.float32
    )
    pair_back = jnp.concatenate(
        [
            keys_back.reshape(sample_count, window_count, key_count, channels),
            values_back.reshape(sample_count, window_count, key_count, channels),
        ],
        axis=-1,
    )
    pair_spread = (
        jnp.zeros((sample_count, row_count + 2 * key_count, 2 * channels), jnp.float32)
        .at[:, offsets]
        .add(pair_back)
    )
    query_full = query_weight.astype(jnp.float32)
    pair_full = pair_weight.astype(jnp.float32)
    normed_back = jnp.dot(query_back, query_full.T, precision=highest)
    query_sum = jnp.einsum("src,srd->cd", normed.astype(jnp.float32), query_back, precision=highest)
    summed = extended(pair_spread.astype(jnp.bfloat16), (("atom", 1),), key_count).astype(
        pair_spread.dtype
    )
    pair_total = pair_spread[:, key_count : key_count + row_count]
    pair_total = pair_total.at[:, :key_count].add(summed[:, :key_count])
    pair_total = pair_total.at[:, row_count - key_count :].add(summed[:, -key_count:])
    pair_sum = jnp.einsum("src,srd->cd", normed.astype(jnp.float32), pair_total, precision=highest)
    normed_back = normed_back + jnp.dot(pair_total, pair_full.T, precision=highest)
    gain_sum = jnp.sum(unit_rows * normed_back, axis=(0, 1))
    unit_back = normed_back * norm_gain
    grad_rows = state_back.astype(jnp.float32) + inverse * (
        unit_back
        - jnp.mean(unit_back, axis=-1, keepdims=True)
        - unit_rows * jnp.mean(unit_back * unit_rows, axis=-1, keepdims=True)
    )
    reduced = lax.psum((gain_sum, query_sum, pair_sum, output_sum, token_sum), ("sample", "atom"))
    total_rows = sample_count * lax.axis_size("sample") * row_count * lax.axis_size("atom")
    rescale = 1.0 / math.sqrt(total_rows)
    return (
        state_out,
        token_rows,
        grad_rows,
        reduced[0] * rescale,
        reduced[1] * rescale,
        reduced[2][:, :channels] * rescale,
        reduced[2][:, channels:] * rescale,
        reduced[3] * rescale,
        reduced[4] * rescale,
    )


def solution(mesh):
    return jax.shard_map(
        on_device,
        mesh=mesh,
        in_specs=(
            P("sample", "atom", None),
            P(),
            P(),
            P(),
            P(),
            P(),
            P(),
            P("atom", None, None, None),
            P("atom"),
            P(),
            P("sample", "atom", None),
            P("sample", "atom", None),
        ),
        out_specs=(
            P("sample", "atom", None),
            P("sample", "atom", None),
            P("sample", "atom", None),
            P(),
            P(),
            P(),
            P(),
            P(),
            P(),
        ),
        check_vma=False,
    )
```

profile of v0, /device:TPU:1, one launch (start us, length us, event | category | flops | bytes accessed | tf_op | source)
XLA Modules:
  0.0 596.7 jit_solution(15851137703708847305)
XLA Ops:
  13.3 4.5 collective-permute-start
  19.8 3.6 collective-permute-start.3
  26.3 44.1 %while.43 = (s32[]{:T(128)}, u32[385]{0:T(512)S(1)}, u32[385]{0:T(512)S(1)}, s32[16384]{0:T(1024)S(1)}, s32[]{:T(128)}, /*index=5*/s32[]{:T(128)}, s32[]{:T(128)}, s32[]{}) while((s32[]{:T(128)}, u32[385]{0:T(512)S(1)}, u32[385]{0:T(512)S(1)}, s32[16384]{0:T(1024)S(1)}, s32[]{:T(128)}, /*index=5*/s32[]{:T(128)}, s32[]{:T(128)}, ...), condition=%wide.region_7.8_spmd.clone, body=%wide.region_6.7_spmd.clone.sunk | while | flops 8343 | bytes 29619 | solution.py:133
  26.4 2.8 gather_fusion
  32.2 2.8 gather_fusion
  35.2 2.8 gather_fusion
  38.1 2.8 gather_fusion
  44.0 2.8 gather_fusion
  46.9 2.8 gather_fusion
  70.5 6.9 %gather_fusion.3 = f32[1024]{0:T(1024)S(1)} fusion(f32[384]{0:T(512)S(1)} %subtract_convert_fusion, s32[1024]{0:T(1024)S(1)} %get-tuple-element.302), kind=kCustom, calls=%fused_computation.3 | custom fusion | bytes 12288 | tf_op jit(solution)/shard_map/jit(_take)/gather | solution.py:148
  79.1 17.0 %gather_fusion.1 = bf16[4096,256]{1,0:T(8,128)(2,1)} fusion(bf16[1280,256]{1,0:T(8,128)(2,1)S(1)} %maximum_bitcast_fusion, s32[4096]{0:T(1024)S(1)} %broadcast_clamp_fusion), kind=kCustom, calls=%fused_computation.1 | custom fusion | bytes 4210688 | tf_op jit(solution)/shard_map/jit(_take)/gather | solution.py:105
  96.1 4.1 copy.30
  107.2 10.7 %fusion.10 = bf16[1,32,32,4,32]{2,4,3,1,0:T(8,128)(2,1)} fusion(bf16[32,128,4,32]{1,3,2,0:T(8,128)(2,1)} %bitcast.140, f32[32,4,32]{2,1,0:T(4,128)S(1)} %get-tuple-element.303, f32[32,4,32,128]{3,2,1,0:T(8,128)} %copy-done.4), kind=kOutput, calls=%fused_computation.34 | convolution fusion | flops 35262592 | bytes 3424256 | tf_op jit(solution)/shard_map/swhqk,swkhd->swqhd/dot_general | solution.py:121
  117.9 2.9 copy.32
  126.7 5.3 gather_fusion.2
  132.0 4.4 multiply_convert_fusion
  142.1 11.1 %fusion.31 = f32[32,4,32,128]{3,2,1,0:T(8,128)} fusion(bf16[32,32,4,32]{1,3,2,0:T(8,128)(2,1)} %copy.38, f32[32,4,32]{2,1,0:T(4,128)S(1)} %copy-done.12, f32[32,4,32,128]{3,2,1,0:T(8,128)} %copy-done.4), kind=kOutput, calls=%fused_computation.65 | convolution fusion | flops 35131520 | bytes 4472832 | tf_op jit(solution)/shard_map/swhqk,swqhd->swkhd/dot_general | solution.py:182
  153.3 4.0 multiply_reduce_fusion
  166.0 3.0 copy.40
  170.9 4.5 pad_maximum_fusion
  175.4 23.2 %scatter_custom_fusion = f32[1280,256]{1,0:T(8,128)S(1)} fusion(s32[4096]{0:T(1024)} %fusion.45, f32[4096,256]{1,0:T(8,128)} %bitcast.138, f32[]{:T(128)} %constant.228.clone.1), kind=kCustom, calls=%fused_computation.50 | custom fusion | flops 1048576 | bytes 1311232 | tf_op jit(solution)/shard_map/scatter-add | solution.py:195
  204.9 39.7 %while.42 = (s32[]{:T(128)}, f32[1,512,768]{2,1,0:T(8,128)}, s32[1024]{0:T(1024)S(1)}, f32[1,1024,768]{2,1,0:T(8,128)}, s32[]{:T(128)}, /*index=5*/s32[1]{0:T(12...) while((s32[]{:T(128)}, f32[1,512,768]{2,1,0:T(8,128)}, ...), condition=%wide.region_5.6_spmd.clone, body=%wide.region_4.5_spmd.clone.sunk | while | flops 151109776 | bytes 4328185 | solution.py:71
  252.6 81.5 %psum.35 = f32[128]{0:T(128)S(1)} all-reduce(f32[128]{0:T(128)S(1)} %get-tuple-element.263), channel_id=1, replica_groups=mesh['sample'=16,'atom'=16] {'sample','atom'}, use_global_device_ids=true, to_apply=%region_13.14 | all-reduce | flops 128 | bytes 1024 | tf_op jit(solution)/shard_map/psum | solution.py:216
  337.9 247.1 %all-reduce.3.cloned.1.call-done = (f32[128,128]{1,0:T(8,128)}, f32[128,256]{1,0:T(8,128)}, f32[128,128]{1,0:T(8,128)}, f32[128,768]{1,0:T(8,128)}) async-done(((f32[128,128]{1,0:T(8,128)}, f32[128,256]{1,0:T(8,128)}, f32[128,128]{1,0:T(8,128)}, f32[128,768]{1,0:T(8,128)}), (f32[128,128]{1,0:T(8,128)}, f32[128,256]{1,0:T(8,128)}, f32[128,128]{1,0:T(8,128)}, ...) | async-done | bytes 655376 | tf_op jit(solution)/shard_map/psum | solution.py:216
  (256 shorter events, 129.8 us)
Async XLA Ops:
  7.2 116.3 %copy-start = (bf16[128,768]{1,0:T(8,128)(2,1)S(1)}, bf16[128,768]{1,0:T(8,128)(2,1)}, u32[]{:S(2)}) copy-start(bf16[128,768]{1,0:T(8,128)(2,1)} %param.26) | copy-start | bytes 589828
  7.2 19.1 %copy-start.2 = (s32[16384]{0:T(1024)S(1)}, s32[16384]{0:T(1024)}, u32[]{:S(2)}) copy-start(s32[16384]{0:T(1024)} %param.29) | copy-start | bytes 196612
  7.2 577.8 %all-reduce.3.cloned.1.call-start = ((), (), s32[]{:S(2)}) async-start(), calls=%async_computation | async-start | bytes 1310720 | tf_op jit(solution)/shard_map/psum | solution.py:216
  13.3 65.7 %collective-permute-start = (bf16[1,128,256]{2,1,0:T(8,128)(2,1)}, bf16[1,128,256]{2,1,0:T(8,128)(2,1)S(1)}, u32[]{:S(2)}, u32[]{:S(2)}) collective-permute-start(bf16[1,128,256]{2,1,0:T(8,128)(2,1)} %get-tuple-element.297), channel_id=1, source_target_pairs={{0,1},{1,2},{2,3},{3,4},{4,5},{5,6},{6,7},{7,8},{8,9},{9,10},{10,1... | collective-permute-start | bytes 196616 | tf_op jit(solution)/shard_map/ppermute | solution.py:20
  17.8 61.2 %collective-permute-start.1 = (bf16[1,128,256]{2,1,0:T(8,128)(2,1)S(1)}, bf16[1,128,256]{2,1,0:T(8,128)(2,1)S(1)}, u32[]{:S(2)}, u32[]{:S(2)}) collective-permute-start(bf16[1,128,256]{2,1,0:T(8,128)(2,1)S(1)} %get-tuple-element.298), channel_id=1, source_target_pairs={{1,0},{2,1},{3,2},{4,3},{5,4},{6,5},{7,6},{8,7},{9,8},{10,9},{11,1... | collective-permute-start | bytes 196616 | tf_op jit(solution)/shard_map/ppermute | solution.py:22
  19.8 106.0 %collective-permute-start.3 = (bf16[1,128,768]{2,1,0:T(8,128)(2,1)}, bf16[1,128,768]{2,1,0:T(8,128)(2,1)}, u32[]{:S(2)}, u32[]{:S(2)}) collective-permute-start(bf16[1,128,768]{2,1,0:T(8,128)(2,1)} %param.31), channel_id=1, source_target_pairs={{0,1},{1,2},{2,3},{3,4},{4,5},{5,6},{6,7},{7,8},{8,9},{9,10},{10,1... | collective-permute-start | bytes 589832 | tf_op jit(solution)/shard_map/ppermute | solution.py:32
  102.0 2.0 copy-start.9
  104.5 2.0 copy-start.4
  117.9 5.3 copy-start.3
  117.9 5.3 copy-start.15
  123.2 2.5 copy-start.8
  123.2 2.5 copy-start.14
  123.5 12.9 %copy-start.7 = (bf16[1,1024,128]{2,1,0:T(8,128)(2,1)}, bf16[1,1024,128]{2,1,0:T(8,128)(2,1)S(1)}, u32[]{:S(2)}) copy-start(bf16[1,1024,128]{2,1,0:T(8,128)(2,1)S(1)} %fusion.15) | copy-start | bytes 786436
  136.4 1.8 copy-start.16
  138.2 4.0 copy-start.12
  153.3 4.0 copy-start.6
  162.2 2.4 copy-start.17
  166.0 3.0 copy-start.5
  199.3 50.7 %collective-permute-start.4 = (bf16[1,128,256]{2,1,0:T(8,128)(2,1)}, bf16[1,128,256]{2,1,0:T(8,128)(2,1)S(1)}, u32[]{:S(2)}, u32[]{:S(2)}) collective-permute-start(bf16[1,128,256]{2,1,0:T(8,128)(2,1)} %get-tuple-element.295), channel_id=1, source_target_pairs={{0,1},{1,2},{2,3},{3,4},{4,5},{5,6},{6,7},{7,8},{8,9},{9,10},{10,1... | collective-permute-start | bytes 196616 | tf_op jit(solution)/shard_map/ppermute | solution.py:20
  201.2 48.8 %collective-permute-start.5 = (bf16[1,128,256]{2,1,0:T(8,128)(2,1)S(1)}, bf16[1,128,256]{2,1,0:T(8,128)(2,1)S(1)}, u32[]{:S(2)}, u32[]{:S(2)}) collective-permute-start(bf16[1,128,256]{2,1,0:T(8,128)(2,1)S(1)} %get-tuple-element.296), channel_id=1, source_target_pairs={{1,0},{2,1},{3,2},{4,3},{5,4},{6,5},{7,6},{8,7},{9,8},{10,9},{11,1... | collective-permute-start | bytes 196616 | tf_op jit(solution)/shard_map/ppermute | solution.py:22
  248.1 87.9 %collective-permute-start.2 = (bf16[1,128,768]{2,1,0:T(8,128)(2,1)}, bf16[1,128,768]{2,1,0:T(8,128)(2,1)}, u32[]{:S(2)}, u32[]{:S(2)}) collective-permute-start(bf16[1,128,768]{2,1,0:T(8,128)(2,1)} %slice.162), channel_id=1, source_target_pairs={{1,0},{2,1},{3,2},{4,3},{5,4},{6,5},{7,6},{8,7},{9,8},{10,9},{11,1... | collective-permute-start | bytes 589832 | tf_op jit(solution)/shard_map/ppermute | solution.py:32
  250.1 1.6 copy-start.10
  251.7 84.3 %copy-start.19 = (f32[128]{0:T(128)S(1)}, f32[128]{0:T(128)}, u32[]{:S(2)}) copy-start(f32[128]{0:T(128)} %slice.119) | copy-start | bytes 1540
  334.1 255.7 %copy-start.1 = (bf16[128,768]{1,0:T(8,128)(2,1)S(1)}, bf16[128,768]{1,0:T(8,128)(2,1)}, u32[]{:S(2)}) copy-start(bf16[128,768]{1,0:T(8,128)(2,1)} %param.26) | copy-start | bytes 589828
  (3 other events, 2.8 us)
Sparse Core Ops, SparseCore 0:
  335.6 249.3 all-reduce.2
where the time goes:
time: 598 us; the launch traced here: 597 us
  waiting for transfers between devices  247 us (41%)
  local copies, waits for them, and re-layouts  128 us (21%)
  blocking collectives  81.5 us (14%)
  matrix products  55 us (9%)
  other arithmetic  52.4 us (9%)
  starting transfers between devices  16.3 us (3%)
  between operations  14.6 us (2%)
    psum x1, waiting for transfers between devices, on_device(): lax.psum((gain_sum, query_sum, pair_sum, output_sum, token_sum), ('sample...  247 us
    psum x1, blocking collectives, on_device(): lax.psum((gain_sum, query_sum, pair_sum, output_sum, token_sum), ('sample...  81.5 us
    gather x15, local copies, waits for them, and re-layouts, on_device(): jnp.searchsorted(atom_token, lower_token + jnp.arange(3 * token_count + 1...  42.6 us
    scatter-add x1, other arithmetic, on_device(): pair_spread = jnp.zeros((sample_count, row_count + 2 * key_count, 2 * cha...  23.2 us
    gather x2, local copies, waits for them, and re-layouts, on_device(): window_pairs = jnp.take(pair_halo, offsets, axis=1)  21.1 us
    dynamic_update_slice x16, local copies, waits for them, and re-layouts, add_block(): return lax.dynamic_update_slice_in_dim(acc, current + contrib, place, 1)  16 us
    dot_general x8, matrix products, add_block(): contrib = jnp.einsum('rk,srw->skw', selector, rows, precision=highest)  12.1 us
  transfers between devices with their start and end apart: 7, of which 1 were waited for; matrix products, arithmetic and copies ran while one was open for 25% of the time, Pallas kernels for 0%

commit v1 on v0

v1 whole, which is shorter than its diff:
```python
import functools
import math

import jax
import jax.numpy as jnp
from jax import lax
from jax.experimental import pallas as pl
from jax.experimental.pallas import tpu as pltpu
from jax.sharding import PartitionSpec as P

MESH = pl.DeviceIdType.MESH
norm_eps = 1e-05
f32 = jnp.float32
bf16 = jnp.bfloat16


def nn(a, b):
    return lax.dot_general(a, b, (((1,), (0,)), ((), ())), preferred_element_type=f32)


def nt(a, b):
    return lax.dot_general(a, b, (((1,), (1,)), ((), ())), preferred_element_type=f32)


def tn(a, b):
    return lax.dot_general(a, b, (((0,), (0,)), ((), ())), preferred_element_type=f32)


def kernel(
    sizes,
    state_hbm,
    gain_ref,
    wq_hbm,
    wk_hbm,
    wv_hbm,
    wo_hbm,
    wt_hbm,
    bias_hbm,
    start_ref,
    token_ref,
    cots_hbm,
    ctok_hbm,
    state_out_hbm,
    rows_out_hbm,
    grad_out_hbm,
    late_out_hbm,
    early_out_hbm,
    state,
    w3,
    wo,
    wt,
    bias,
    cots,
    ctok,
    ctok_low,
    halo,
    unit,
    inverse,
    normed,
    queries,
    kvf,
    kvw,
    probs,
    attended,
    state_out,
    sel_cat,
    sel_t,
    sel_tlow,
    tokens_back,
    inv_own,
    silu,
    active,
    state_back,
    attended_back,
    low_part,
    high_part,
    rows_out,
    shift,
    spread,
    query_back,
    spread_low,
    nback,
    nback_send,
    nback_recv,
    grad_out,
    e_src,
    e_rx1,
    e_sum,
    e_rx2,
    e_fin,
    l_src,
    l_rx1,
    l_sum,
    l_rx2,
    l_fin,
    head_mask,
    load_sem,
    out_sem,
    send_sem,
    recv_sem,
):
    A, B, rows, channels, windows, heads, qw, keys, toks, width = sizes
    margin = keys // 2 + qw // 2
    full = rows + 2 * margin
    span = keys + 2 * qw
    head_dim = channels // heads
    factor = head_dim ** (-0.5)
    fold = 2 * channels // A
    half = channels // A
    me = lax.axis_index("atom")
    smp = lax.axis_index("sample")
    left = {"atom": lax.rem(me + A - 1, A)}
    right = {"atom": lax.rem(me + 1, A)}

    def load(src, dst, index):
        return pltpu.make_async_copy(src, dst, load_sem.at[index])

    loads = [
        load(state_hbm.at[0], state, 0),
        load(wq_hbm, w3.at[:, pl.ds(0, channels)], 1),
        load(wk_hbm, w3.at[:, pl.ds(channels, channels)], 2),
        load(wv_hbm, w3.at[:, pl.ds(2 * channels, channels)], 3),
        load(bias_hbm, bias, 4),
        load(wo_hbm, wo, 5),
        load(wt_hbm, wt, 6),
        load(cots_hbm.at[0], cots, 7),
        load(ctok_hbm.at[0], ctok, 8),
    ]
    for copy in loads:
        copy.start()

    barrier = pltpu.get_barrier_semaphore()

    def greet(d, _):
        pl.semaphore_signal(
            barrier, inc=1, device_id={"atom": lax.rem(me + d, A)}, device_id_type=MESH
        )
        return 0

    def greet_sample(d, _):
        pl.semaphore_signal(
            barrier, inc=1, device_id={"sample": lax.rem(smp + d, B)}, device_id_type=MESH
        )
        return 0

    lax.fori_loop(1, A, greet, 0)
    lax.fori_loop(1, B, greet_sample, 0)

    def send(src, dst, index, device):
        return pltpu.make_async_remote_copy(
            src_ref=src,
            dst_ref=dst,
            send_sem=send_sem.at[index],
            recv_sem=recv_sem.at[index],
            device_id=device,
            device_id_type=MESH,
        )

    def wait_bytes(ref, sem):
        pltpu.make_async_copy(ref, ref, sem).wait()

    def norm(x):
        x = x.astype(f32)
        average = jnp.mean(x, axis=-1, keepdims=True)
        centred = x - average
        variance = jnp.mean(centred * centred, axis=-1, keepdims=True)
        inv = lax.rsqrt(variance + norm_eps)
        unit_rows = centred * inv
        return unit_rows, inv, (unit_rows * gain_ref[...]).astype(bf16)

    for index in range(4):
        loads[index].wait()

    lanes = lax.broadcasted_iota(jnp.int32, (keys, channels), 1)
    subs = lax.broadcasted_iota(jnp.int32, (keys, channels), 0)
    head_mask[...] = jnp.where(subs // qw == lanes // head_dim, 1.0, 0.0).astype(bf16)

    block = 256

    def project(c, _):
        r = pl.multiple_of(c * block, block)
        unit_rows, inv, low = norm(state[pl.ds(r, block), :])
        unit[pl.ds(margin + r, block), :] = unit_rows
        inverse[pl.ds(r, block), :] = jnp.broadcast_to(inv, (block, channels))
        normed[pl.ds(margin + r, block), :] = low
        qkv = nn(low, w3[...]).astype(bf16)
        queries[pl.ds(r, block), :] = qkv[:, :channels]
        kvf[0, pl.ds(margin + r, block), :] = qkv[:, channels : 2 * channels].astype(f32)
        kvf[1, pl.ds(margin + r, block), :] = qkv[:, 2 * channels :].astype(f32)
        return 0

    lax.fori_loop(0, rows // block, project, 0)

    pl.semaphore_wait(barrier, A + B - 2)

    halo_left = send(
        state_hbm.at[0, pl.ds(rows - margin, margin), :], halo.at[0], 0, right
    )
    halo_right = send(state_hbm.at[0, pl.ds(0, margin), :], halo.at[1], 1, left)
    tokens_up = send(ctok_hbm.at[0], ctok_low, 2, right)
    halo_left.start()
    halo_right.start()
    tokens_up.start()

    spread[...] = jnp.zeros((2, full, channels), f32)
    for slot in range(4):
        shift[slot, pl.ds(0, 2 * qw), :] = jnp.zeros((2 * qw, channels), f32)
        shift[slot, pl.ds(2 * qw + keys, 2 * qw), :] = jnp.zeros((2 * qw, channels), f32)

    per_tile = rows // 128
    base = (me * toks).astype(f32)
    lower = base - toks
    sub_id = subs.astype(f32)
    lane_id = lanes.astype(f32)
    count_own = jnp.zeros((toks, 128), f32)
    count_low = jnp.zeros((toks, 128), f32)
    for r in range(per_tile):
        row = token_ref[pl.ds(me * per_tile + r, 1), :].astype(f32)
        spot = jnp.broadcast_to(row, (128, 128))
        hit = jnp.where(spot - base == sub_id, 1.0, 0.0)
        count_own = count_own + hit
        sel_t[:, pl.ds(r * 128, 128)] = hit.astype(bf16)
        if r < 2:
            hit = jnp.where(spot - lower == sub_id, 1.0, 0.0)
            count_low = count_low + hit
            sel_tlow[:, pl.ds(r * 128, 128)] = hit.astype(bf16)
        column = spot.T - lower
        sel_cat[pl.ds(r * 128, 128), pl.ds(0, 128)] = jnp.where(
            column == lane_id, 1.0, 0.0
        ).astype(bf16)
        sel_cat[pl.ds(r * 128, 128), pl.ds(128, 128)] = jnp.where(
            column == lane_id + toks, 1.0, 0.0
        ).astype(bf16)
    has_above = jnp.where(me < A - 1, 1.0, 0.0)
    above = jnp.minimum(me + 1, A - 1) * per_tile
    for r in range(2):
        row = token_ref[pl.ds(above + r, 1), :].astype(f32)
        spot = jnp.broadcast_to(row, (128, 128))
        count_own = count_own + jnp.where(spot - base == sub_id, has_above, 0.0)
    has_below = jnp.where(me > 0, 1.0, 0.0)
    below = jnp.maximum(me - 1, 0) * per_tile
    for r in range(per_tile):
        row = token_ref[pl.ds(below + r, 1), :].astype(f32)
        spot = jnp.broadcast_to(row, (128, 128))
        count_low = count_low + jnp.where(spot - lower == sub_id, has_below, 0.0)

    def inverted(count):
        total = jnp.sum(count, axis=-1, keepdims=True)
        return jnp.where(total > 0.0, 1.0 / jnp.maximum(total, 1.0), 0.0)

    inverse_own = inverted(count_own)
    inverse_low = inverted(count_low)
    inv_own[...] = jnp.broadcast_to(inverse_own, (toks, 128))
    loads[8].wait()
    tokens_back[pl.ds(toks, toks), :] = (ctok[...].astype(f32) * inverse_own).astype(bf16)

    first_atom = me * rows
    last_base = A * rows - span

    def spread_heads(x):
        return jnp.concatenate([x] * heads, axis=0) * head_mask[...]

    def gather_heads(x):
        lane = lax.broadcasted_iota(jnp.int32, (qw, channels), 1)
        out = x[0:qw]
        for h in range(1, heads):
            out = jnp.where(lane >= h * head_dim, x[h * qw : (h + 1) * qw], out)
        return out

    def forward(w):
        place = jnp.clip(start_ref[w] - first_atom + margin, 0, full - keys)
        k = kvf[0, pl.ds(place, keys), :].astype(bf16)
        v = kvf[1, pl.ds(place, keys), :].astype(bf16)
        kvw[w, :, pl.ds(0, channels)] = k
        kvw[w, :, pl.ds(channels, channels)] = v
        q0 = pl.multiple_of(w * qw, qw)
        q = spread_heads(queries[pl.ds(q0, qw), :])
        s = nt(q, k) * factor + bias[w]
        e = jnp.exp(s - jnp.max(s, axis=-1, keepdims=True))
        p = (e / jnp.sum(e, axis=-1, keepdims=True)).astype(bf16)
        probs[w] = p
        attended[pl.ds(q0, qw), :] = gather_heads(nn(p, v)).astype(bf16)

    near = (margin + qw - 1) // qw
    loads[4].wait()

    def forward_pair(i, _):
        for k in range(2):
            forward(lax.rem(2 * i + k + near, windows))
        return 0

    inner = (windows - 2 * near) // 2
    lax.fori_loop(0, inner, forward_pair, 0)

    halo_left.wait_recv()
    halo_right.wait_recv()
    for side in range(2):
        there = (me > 0) if side == 0 else (me < A - 1)
        at = 0 if side == 0 else margin + rows
        keep = jnp.where(there, 1.0, 0.0)
        x = jnp.where(jnp.full((margin, channels), keep) > 0.0, halo[side].astype(f32), 0.0)
        unit_rows, _, low = norm(x)
        unit[pl.ds(at, margin), :] = unit_rows
        normed[pl.ds(at, margin), :] = low
        kv = nn(low, w3[:, channels:]).astype(bf16).astype(f32)
        kvf[0, pl.ds(at, margin), :] = kv[:, :channels]
        kvf[1, pl.ds(at, margin), :] = kv[:, channels:]

    lax.fori_loop(inner, windows // 2, forward_pair, 0)

    tokens_up.wait_recv()
    tokens_back[pl.ds(0, toks), :] = (ctok_low[...].astype(f32) * inverse_low).astype(bf16)
    for index in range(5, 8):
        loads[index].wait()

    def token_part(c):
        r = c * block if isinstance(c, int) else pl.multiple_of(c * block, block)
        here = pl.ds(r, block)
        out = (state[here, :].astype(f32) + nn(attended[here, :], wo[...])).astype(bf16)
        state_out[here, :] = out
        before = nn(out, wt[...])
        sigma = 0.5 * jnp.tanh(0.5 * before) + 0.5
        act = before * sigma
        silu[here, :] = act.astype(bf16)
        slope = sigma + act - act * sigma
        per_atom = nn(sel_cat[here, :], tokens_back[...])
        back = (per_atom * slope).astype(bf16)
        active[here, :] = back
        sback = (cots[here, :].astype(f32) + nt(back, wt[...])).astype(bf16)
        state_back[here, :] = sback
        attended_back[here, :] = nt(sback, wo[...]).astype(bf16)

    token_part(0)
    low_part[...] = nn(sel_tlow[...], silu[pl.ds(0, 256), :]).astype(bf16)
    part_down = send(low_part, high_part, 3, left)
    part_down.start()
    lax.fori_loop(1, rows // block, lambda c, _: (token_part(c), 0)[1], 0)

    def store(src, dst, index):
        return pltpu.make_async_copy(src, dst, out_sem.at[index])

    out_state = store(state_out, state_out_hbm.at[0], 0)
    out_state.start()

    def folded(x):
        x = x.reshape(A, half, x.shape[-1])
        mid = x.shape[-1] // 2
        return jnp.concatenate([x[..., :mid], x[..., mid:]], axis=1)

    def stacked(x, y):
        return jnp.concatenate(
            [x.reshape(A, half, channels), y.reshape(A, half, channels)], axis=1
        )

    token_sum = tn(state_out[...], active[...])
    e_src[:, :, pl.ds(0, width // 2)] = folded(token_sum).astype(bf16)
    output_sum = tn(attended[...], state_back[...])
    output_high = output_sum.astype(bf16).astype(f32)
    e_src[:, :, pl.ds(width // 2, channels)] = stacked(
        output_high, output_sum - output_high
    ).astype(bf16)

    def scatter(src, rx, index):
        def one(d, _):
            peer = lax.rem(me + d, A)
            send(src.at[peer], rx.at[d], index, {"atom": peer}).start()
            return 0

        lax.fori_loop(1, A, one, 0)

    def scattered(src, rx, part, rx2, index):
        wait_bytes(rx.at[pl.ds(1, A - 1)], recv_sem.at[index])
        total = src[me].astype(f32)
        for d in range(1, A):
            total = total + rx[d].astype(f32)
        low = total.astype(bf16)
        part[...] = low
        rx2[smp] = low

    def exchange(part, rx2, index):
        def one(d, _):
            peer = lax.rem(smp + d, B)
            send(part, rx2.at[smp], index, {"sample": peer}).start()
            return 0

        lax.fori_loop(1, B, one, 0)

    def exchanged(rx2, fin, index):
        wait_bytes(rx2.at[pl.ds(0, B - 1)], recv_sem.at[index])
        total = rx2[0].astype(f32)
        for d in range(1, B):
            total = total + rx2[d].astype(f32)
        fin[me] = total.astype(bf16)

    def gather(fin, index):
        def one(d, _):
            peer = lax.rem(me + d, A)
            send(fin.at[me], fin.at[me], index, {"atom": peer}).start()
            return 0

        lax.fori_loop(1, A, one, 0)

    def gathered(fin, index):
        wait_bytes(fin.at[pl.ds(0, A - 1)], recv_sem.at[index])

    scatter(e_src, e_rx1, 4)

    def backward(w, slot):
        base_atom = jnp.clip(first_atom + w * qw - margin, 0, last_base)
        off = jnp.clip(start_ref[w] - base_atom, 0, 2 * qw)
        kv = kvw[w]
        q0 = pl.multiple_of(w * qw, qw)
        q = spread_heads(queries[pl.ds(q0, qw), :])
        da = spread_heads(attended_back[pl.ds(q0, qw), :])
        p = probs[w]
        pf = p.astype(f32)
        weighted = pf * nt(da, kv[:, channels:])
        ds = (weighted - pf * jnp.sum(weighted, axis=-1, keepdims=True)).astype(bf16)
        dq = gather_heads(nn(ds, kv[:, :channels]))
        query_back[pl.ds(q0, qw), :] = (dq * factor).astype(bf16)
        to = pl.ds(pl.multiple_of(base_atom - first_atom + margin, 16), span)
        for part, rows_back in enumerate((tn(ds, q) * factor, tn(p, da))):
            shift[2 * slot + part, pl.ds(2 * qw, keys), :] = rows_back
            moved = shift[2 * slot + part, pl.ds(2 * qw - off, span), :]
            spread[part, to, :] = spread[part, to, :] + moved

    def backward_pair(i, _):
        for k in range(2):
            backward(2 * i + k, k)
        return 0

    lax.fori_loop(0, windows // 4, backward_pair, 0)
    scattered(e_src, e_rx1, e_sum, e_rx2, 4)
    exchange(e_sum, e_rx2, 5)
    lax.fori_loop(windows // 4, windows // 2, backward_pair, 0)
    exchanged(e_rx2, e_fin, 5)
    gather(e_fin, 6)

    spread_low[:, pl.ds(0, channels)] = spread[0].astype(bf16)
    spread_low[:, pl.ds(channels, channels)] = spread[1].astype(bf16)
    nback[...] = nt(spread_low[...], w3[:, channels:])
    nback_send[0] = nback[pl.ds(0, margin), :].astype(bf16)
    nback_send[1] = nback[pl.ds(margin + rows, margin), :].astype(bf16)
    back_left = send(nback_send.at[0], nback_recv.at[1], 7, left)
    back_right = send(nback_send.at[1], nback_recv.at[0], 8, right)
    back_left.start()
    back_right.start()
    own = pl.ds(margin, rows)
    nback[own, :] = nback[own, :] + nt(query_back[...], w3[:, :channels])
    query_sum = tn(normed[own, :], query_back[...])
    pair_sum = tn(normed[...], spread_low[...])
    gain_part = jnp.sum((unit[...] * nback[...]).reshape(full // 8, 8, channels), axis=0)
    gain_rows = jnp.concatenate([gain_part, jnp.zeros((channels - 8, channels), f32)], axis=0)
    l_src[:, :, pl.ds(0, channels)] = stacked(query_sum, pair_sum[:, :channels]).astype(bf16)
    l_src[:, :, pl.ds(channels, channels)] = stacked(pair_sum[:, channels:], gain_rows).astype(
        bf16
    )
    scatter(l_src, l_rx1, 9)

    part_down.wait_recv()
    own_part = nn(sel_t[...], silu[...])
    rows_out[...] = (
        (own_part + high_part[...].astype(f32)) * inv_own[:, pl.ds(0, 1)]
    ).astype(bf16)
    out_rows = store(rows_out, rows_out_hbm.at[0], 1)
    out_rows.start()

    def norm_back(r, count, extra):
        here = pl.ds(r, count)
        there = pl.ds(margin + r, count)
        nb = nback[there, :]
        if extra is not None:
            nb = nb + extra
        ub = nb * gain_ref[...]
        un = unit[there, :]
        grad_out[here, :] = state_back[here, :].astype(f32) + inverse[here, :] * (
            ub
            - jnp.mean(ub, axis=-1, keepdims=True)
            - un * jnp.mean(ub * un, axis=-1, keepdims=True)
        )

    for r in range(0, rows - 2 * margin, 216):
        norm_back(margin + r, min(216, rows - 2 * margin - r), None)
    back_left.wait_recv()
    back_right.wait_recv()
    norm_back(0, margin, nback_recv[0].astype(f32))
    norm_back(rows - margin, margin, nback_recv[1].astype(f32))
    out_grad = store(grad_out, grad_out_hbm.at[0], 2)
    out_grad.start()

    scattered(l_src, l_rx1, l_sum, l_rx2, 9)
    exchange(l_sum, l_rx2, 10)
    gathered(e_fin, 6)
    out_early = store(e_fin, early_out_hbm, 3)
    out_early.start()
    exchanged(l_rx2, l_fin, 10)
    gather(l_fin, 11)
    gathered(l_fin, 11)
    out_late = store(l_fin, late_out_hbm, 4)
    out_late.start()

    for copy in (halo_left, halo_right, tokens_up, part_down, back_left, back_right):
        copy.wait_send()
    for index, ref, count in (
        (4, e_rx1, A),
        (5, e_rx2, B),
        (6, e_fin, A),
        (9, l_rx1, A),
        (10, l_rx2, B),
        (11, l_fin, A),
    ):
        wait_bytes(ref.at[pl.ds(0, count - 1)], send_sem.at[index])
    for copy in (out_state, out_rows, out_grad, out_early, out_late):
        copy.wait()


def on_device(
    A,
    B,
    atom_state,
    norm_gain,
    query_weight,
    key_weight,
    value_weight,
    out_weight,
    token_weight,
    pair_bias,
    key_start,
    atom_token,
    cotangent_state,
    cotangent_tokens,
):
    _, rows, channels = atom_state.shape
    windows, heads, qw, keys = pair_bias.shape
    toks, width = cotangent_tokens.shape[1:]
    sizes = (A, B, rows, channels, windows, heads, qw, keys, toks, width)
    margin = keys // 2 + qw // 2
    full = rows + 2 * margin
    span = keys + 2 * qw
    fold = 2 * channels // A
    half = channels // A
    early = width // 2 + channels
    late = 2 * channels
    any_spec = pl.BlockSpec(memory_space=pl.ANY)
    vmem = pl.BlockSpec(memory_space=pltpu.VMEM)
    smem = pl.BlockSpec(memory_space=pltpu.SMEM)
    V = pltpu.VMEM
    DMA = pltpu.SemaphoreType.DMA
    outs = pl.pallas_call(
        functools.partial(kernel, sizes),
        out_shape=(
            jax.ShapeDtypeStruct((1, rows, channels), bf16),
            jax.ShapeDtypeStruct((1, toks, width), bf16),
            jax.ShapeDtypeStruct((1, rows, channels), f32),
            jax.ShapeDtypeStruct((A, fold, late), bf16),
            jax.ShapeDtypeStruct((A, fold, early), bf16),
        ),
        in_specs=[any_spec, vmem]
        + [any_spec] * 6
        + [smem, vmem]
        + [any_spec] * 2,
        out_specs=(any_spec,) * 5,
        scratch_shapes=[
            V((rows, channels), bf16),
            V((channels, 3 * channels), bf16),
            V((channels, channels), bf16),
            V((channels, width), bf16),
            V((windows, heads * qw, keys), f32),
            V((rows, channels), bf16),
            V((toks, width), bf16),
            V((toks, width), bf16),
            V((2, margin, channels), bf16),
            V((full, channels), f32),
            V((rows, channels), f32),
            V((full, channels), bf16),
            V((rows, channels), bf16),
            V((2, full, channels), f32),
            V((windows, keys, 2 * channels), bf16),
            V((windows, heads * qw, keys), bf16),
            V((rows, channels), bf16),
            V((rows, channels), bf16),
            V((rows, 2 * toks), bf16),
            V((toks, rows), bf16),
            V((toks, 256), bf16),
            V((2 * toks, width), bf16),
            V((toks, 128), f32),
            V((rows, width), bf16),
            V((rows, width), bf16),
            V((rows, channels), bf16),
            V((rows, channels), bf16),
            V((toks, width), bf16),
            V((toks, width), bf16),
            V((toks, width), bf16),
            V((4, keys + 4 * qw, channels), f32),
            V((2, full, channels), f32),
            V((rows, channels), bf16),
            V((full, 2 * channels), bf16),
            V((full, channels), f32),
            V((2, margin, channels), bf16),
            V((2, margin, channels), bf16),
            V((rows, channels), f32),
            V((A, fold, early), bf16),
            V((A, fold, early), bf16),
            V((fold, early), bf16),
            V((B, fold, early), bf16),
            V((A, fold, early), bf16),
            V((A, fold, late), bf16),
            V((A, fold, late), bf16),
            V((fold, late), bf16),
            V((B, fold, late), bf16),
            V((A, fold, late), bf16),
            V((keys, channels), bf16),
            DMA((9,)),
            DMA((5,)),
            DMA((12,)),
            DMA((12,)),
        ],
        compiler_params=pltpu.CompilerParams(
            collective_id=0, has_side_effects=True, vmem_limit_bytes=48 * 1024 * 1024
        ),
        name="atom_block",
    )(
        atom_state,
        norm_gain.reshape(1, channels),
        query_weight,
        key_weight,
        value_weight,
        out_weight,
        token_weight,
        pair_bias.reshape(windows, heads * qw, keys),
        key_start,
        atom_token.reshape(-1, 128),
        cotangent_state,
        cotangent_tokens,
    )
    state_out, token_rows, grad_state, late_sum, early_sum = outs
    rescale = 1.0 / math.sqrt(B * A * rows)
    late_sum = late_sum.astype(f32) * rescale
    early_sum = early_sum.astype(f32) * rescale
    square = (channels, channels)
    grad_query = late_sum[:, :half, :channels].reshape(square)
    grad_key = late_sum[:, half:, :channels].reshape(square)
    grad_value = late_sum[:, :half, channels:].reshape(square)
    grad_gain = jnp.sum(late_sum[:, half:, channels:], axis=(0, 1))
    grad_token = jnp.concatenate(
        [early_sum[:, :half, : width // 2], early_sum[:, half:, : width // 2]], axis=-1
    ).reshape(channels, width)
    grad_output = (
        early_sum[:, :half, width // 2 :] + early_sum[:, half:, width // 2 :]
    ).reshape(square)
    return (
        state_out,
        token_rows,
        grad_state,
        grad_gain,
        grad_query,
        grad_key,
        grad_value,
        grad_output,
        grad_token,
    )


def solution(mesh):
    return jax.shard_map(
        functools.partial(on_device, mesh.shape["atom"], mesh.shape["sample"]),
        mesh=mesh,
        in_specs=(
            P("sample", "atom", None),
            P(),
            P(),
            P(),
            P(),
            P(),
            P(),
            P("atom", None, None, None),
            P("atom"),
            P(),
            P("sample", "atom", None),
            P("sample", "atom", None),
        ),
        out_specs=(
            P("sample", "atom", None),
            P("sample", "atom", None),
            P("sample", "atom", None),
            P(),
            P(),
            P(),
            P(),
            P(),
            P(),
        ),
        check_vma=False,
    )
```

time: 598 us -> 81.2 us (0.14)
  waiting for transfers between devices: 247 us -> 0 us
  local copies, waits for them, and re-layouts: 128 us -> 12.7 us
  blocking collectives: 81.5 us -> 0 us
  Pallas kernels: 0 us -> 64.6 us
  matrix products: 55 us -> 0 us
  other arithmetic: 52.4 us -> 2.69 us
  starting transfers between devices: 16.3 us -> 0 us
  between operations: 14.6 us -> 0.7 us
    psum x1 -> x0, waiting for transfers between devices: 247 us -> none  [on_device(): lax.psum((gain_sum, query_sum, pair_sum, output_sum, token_sum), ('sample...]
    psum x1 -> x0, blocking collectives: 81.5 us -> none  [on_device(): lax.psum((gain_sum, query_sum, pair_sum, output_sum, token_sum), ('sample...]
    gather x19 -> x0, local copies, waits for them, and re-layouts: 75.8 us -> none  [the longest x15 42.6 us: on_device(): jnp.searchsorted(atom_token, lower_token + jnp.arange(3 * token_count + 1...]
    pallas_call x0 -> x1, Pallas kernels: none -> 64.6 us  [on_device(): pl.pallas_call(functools.partial(kernel, sizes), out_shape=(jax.ShapeDtyp...]
    dot_general x26 -> x0, matrix products: 55 us -> none  [the longest x8 12.1 us: add_block(): contrib = jnp.einsum('rk,srw->skw', selector, rows, precision=highest)]
    scatter-add x3 -> x0, other arithmetic: 23.2 us -> none  [the longest x1 23.2 us: on_device(): pair_spread = jnp.zeros((sample_count, row_count + 2 * key_count, 2 * cha...]
    ppermute x6 -> x0, starting transfers between devices: 16.3 us -> none  [the longest x2 6.42 us: extended(): lax.ppermute(tail, axis, [(i, (i + 1) % count) for i in range(ends)])]
    dynamic_update_slice x16 -> x0, local copies, waits for them, and re-layouts: 16 us -> none  [add_block(): return lax.dynamic_update_slice_in_dim(acc, current + contrib, place, 1)]
  transfers between devices with their start and end apart: 7 -> 0, of which waited for: 1 -> 0; matrix products, arithmetic and copies ran while one was open for 25% -> 0% of each run, Pallas kernels for 0% -> 0%
where the time goes in v1:
time: 81.2 us; the launch traced here: 80.7 us
  Pallas kernels  64.6 us (80%)
  local copies, waits for them, and re-layouts  12.7 us (16%)
  other arithmetic  2.69 us (3%)
    pallas_call x1, Pallas kernels, on_device(): pl.pallas_call(functools.partial(kernel, sizes), out_shape=(jax.ShapeDtyp...  64.6 us
    unnamed x27, local copies, waits for them, and re-layouts  12.7 us

profile of v1, /device:TPU:1, one launch (start us, length us, event | category | flops | bytes accessed | tf_op | source)
XLA Modules:
  0.0 80.7 jit_solution(9081594925222646220)
XLA Ops:
  0.6 0.0 copy-start
  0.7 1.6 %copy-done = f32[32,4,32,128]{3,2,1,0:T(8,128)S(1)} copy-done((f32[32,4,32,128]{3,2,1,0:T(8,128)S(1)}, f32[32,4,32,128]{3,2,1,0:T(8,128)}, u32[]{:S(2)}) %copy-start) | copy-done | bytes 2097176
  2.2 0.0 copy-start.1
  2.2 0.9 %copy-done.1 = bf16[1,1024,128]{2,1,0:T(8,128)(2,1)S(1)} copy-done((bf16[1,1024,128]{2,1,0:T(8,128)(2,1)S(1)}, bf16[1,1024,128]{2,1,0:T(8,128)(2,1)}, u32[]{:S(2)}) %copy-start.1) | copy-done | bytes 262168
  3.2 0.0 copy-start.2
  3.2 0.9 %copy-done.2 = bf16[1,1024,128]{2,1,0:T(8,128)(2,1)S(1)} copy-done((bf16[1,1024,128]{2,1,0:T(8,128)(2,1)S(1)}, bf16[1,1024,128]{2,1,0:T(8,128)(2,1)}, u32[]{:S(2)}) %copy-start.2) | copy-done | bytes 262168
  4.1 0.0 copy-start.3
  4.1 0.9 %copy-done.3 = bf16[128,768]{1,0:T(8,128)(2,1)S(1)} copy-done((bf16[128,768]{1,0:T(8,128)(2,1)S(1)}, bf16[128,768]{1,0:T(8,128)(2,1)}, u32[]{:S(2)}) %copy-start.3) | copy-done | bytes 196632
  5.1 0.9 %copy-done.4 = bf16[1,128,768]{2,1,0:T(8,128)(2,1)S(1)} copy-done((bf16[1,128,768]{2,1,0:T(8,128)(2,1)S(1)}, bf16[1,128,768]{2,1,0:T(8,128)(2,1)}, u32[]{:S(2)}) %copy-start.4) | copy-done | bytes 196632
  6.0 0.8 %copy-done.5 = s32[16384]{0:T(1024)S(1)} copy-done((s32[16384]{0:T(1024)S(1)}, s32[16384]{0:T(1024)}, u32[]{:S(2)}) %copy-start.5) | copy-done | bytes 65560
  6.8 0.8 copy-done.6
  7.6 0.8 copy-done.7
  8.4 0.8 copy-done.8
  9.1 0.8 copy-done.9
  9.9 0.7 copy-done.10
  10.5 0.7 copy-done.11
  11.2 64.6 %atom_block.1 = (bf16[1,1024,128]{2,1,0:T(8,128)(2,1)S(1)}, bf16[1,128,768]{2,1,0:T(8,128)(2,1)S(1)}, f32[1,1024,128]{2,1,0:T(8,128)S(1)}, bf16[16,16,256]{2,1,0:T(8,128)(2,1)S(1)}, bf16[16,16,512]{2,1,0:T(8,128)(2,1)S(1)}) custom-call(bf16[1,1024,128]{2,1,0:T(8,128)(2,1)S(1)} %copy-done.1, f32[1,128]{1,0:T(1,128)S(1)} %bitcast.15, ...), custom_call_target="tpu_custom_call" | custom-call | tf_op jit(solution)/shard_map/atom_block/pallas_call | solution.py:549
  75.8 1.2 %slice_bitcast_fusion = (f32[128,128]{1,0:T(8,128)}, f32[128,128]{1,0:T(8,128)}, f32[128,128]{1,0:T(8,128)}, f32[128]{0:T(128)}) fusion(f32[16,16,256]{2,1,0:T(8,128)S(1)} %convert_multiply_fusion.1), kind=kLoop, calls=%fused_computation.5 | loop fusion | flops 16256 | bytes 459264 | tf_op jit(solution)/shard_map/reshape | solution.py:643
  77.0 0.1 convert_multiply_fusion
  77.1 0.7 fusion
  77.7 0.8 maximum_bitcast_fusion
  78.5 0.7 copy.24
  79.2 0.7 copy.25
  79.9 0.8 copy.26
  (10 shorter events, 0.1 us)
Async XLA Ops:
  0.6 1.6 %copy-start = (f32[32,4,32,128]{3,2,1,0:T(8,128)S(1)}, f32[32,4,32,128]{3,2,1,0:T(8,128)}, u32[]{:S(2)}) copy-start(f32[32,4,32,128]{3,2,1,0:T(8,128)} %param.19) | copy-start | bytes 6291460
  2.2 0.9 %copy-start.1 = (bf16[1,1024,128]{2,1,0:T(8,128)(2,1)S(1)}, bf16[1,1024,128]{2,1,0:T(8,128)(2,1)}, u32[]{:S(2)}) copy-start(bf16[1,1024,128]{2,1,0:T(8,128)(2,1)} %state_hbm.1) | copy-start | bytes 786436
  3.2 0.9 %copy-start.2 = (bf16[1,1024,128]{2,1,0:T(8,128)(2,1)S(1)}, bf16[1,1024,128]{2,1,0:T(8,128)(2,1)}, u32[]{:S(2)}) copy-start(bf16[1,1024,128]{2,1,0:T(8,128)(2,1)} %cots_hbm.1) | copy-start | bytes 786436
  4.1 0.9 %copy-start.3 = (bf16[128,768]{1,0:T(8,128)(2,1)S(1)}, bf16[128,768]{1,0:T(8,128)(2,1)}, u32[]{:S(2)}) copy-start(bf16[128,768]{1,0:T(8,128)(2,1)} %wt_hbm.1) | copy-start | bytes 589828
  5.1 0.9 %copy-start.4 = (bf16[1,128,768]{2,1,0:T(8,128)(2,1)S(1)}, bf16[1,128,768]{2,1,0:T(8,128)(2,1)}, u32[]{:S(2)}) copy-start(bf16[1,128,768]{2,1,0:T(8,128)(2,1)} %ctok_hbm.1) | copy-start | bytes 589828
  6.0 0.8 %copy-start.5 = (s32[16384]{0:T(1024)S(1)}, s32[16384]{0:T(1024)}, u32[]{:S(2)}) copy-start(s32[16384]{0:T(1024)} %param.21) | copy-start | bytes 196612
  6.8 0.8 copy-start.6
  7.6 0.8 copy-start.7
  8.4 0.8 copy-start.8
  9.1 0.8 copy-start.9
  9.9 0.7 copy-start.10
  10.5 0.7 copy-start.11

commit v2 on v1

--- a/solution.py
+++ b/solution.py
@@ -29,15 +29,15 @@
 def kernel(
     sizes,
     state_hbm,
-    gain_ref,
+    gain_hbm,
     wq_hbm,
     wk_hbm,
     wv_hbm,
     wo_hbm,
     wt_hbm,
     bias_hbm,
-    start_ref,
-    token_ref,
+    start_hbm,
+    token_hbm,
     cots_hbm,
     ctok_hbm,
     state_out_hbm,
@@ -45,6 +45,9 @@
     grad_out_hbm,
     late_out_hbm,
     early_out_hbm,
+    gain_ref,
+    start_ref,
+    token_ref,
     state,
     w3,
     wo,
@@ -94,6 +97,7 @@
     l_rx2,
     l_fin,
     head_mask,
+    mean_mat,
     load_sem,
     out_sem,
     send_sem,
@@ -112,6 +116,10 @@
     left = {"atom": lax.rem(me + A - 1, A)}
     right = {"atom": lax.rem(me + 1, A)}
 
+    tile = rows // 128
+    below = pl.multiple_of(jnp.maximum(me - 1, 0) * tile, 8)
+    above = pl.multiple_of(jnp.minimum(me + 1, A - 1) * tile, 8)
+
     def load(src, dst, index):
         return pltpu.make_async_copy(src, dst, load_sem.at[index])
 
@@ -125,10 +133,12 @@
         load(wt_hbm, wt, 6),
         load(cots_hbm.at[0], cots, 7),
         load(ctok_hbm.at[0], ctok, 8),
+        load(gain_hbm, gain_ref, 9),
+        load(start_hbm, start_ref, 10),
+        load(token_hbm.at[pl.ds(below, tile)], token_ref.at[pl.ds(0, tile)], 11),
+        load(token_hbm.at[pl.ds(pl.multiple_of(me * tile, 8), tile)], token_ref.at[pl.ds(tile, tile)], 12),
+        load(token_hbm.at[pl.ds(above, tile)], token_ref.at[pl.ds(2 * tile, tile)], 13),
     ]
-    for copy in loads:
-        copy.start()
-
     barrier = pltpu.get_barrier_semaphore()
 
     def greet(d, _):
@@ -145,6 +155,9 @@
 
     lax.fori_loop(1, A, greet, 0)
     lax.fori_loop(1, B, greet_sample, 0)
+
+    for copy in loads:
+        copy.start()
 
     def send(src, dst, index, device):
         return pltpu.make_async_remote_copy(
@@ -160,28 +173,37 @@
         pltpu.make_async_copy(ref, ref, sem).wait()
 
     def norm(x):
-        x = x.astype(f32)
-        average = jnp.mean(x, axis=-1, keepdims=True)
-        centred = x - average
-        variance = jnp.mean(centred * centred, axis=-1, keepdims=True)
+        average = nn(x, mean_mat[pl.ds(0, channels), pl.ds(0, channels)])
+        centred = x.astype(f32) - average
+        square = (centred * centred).astype(bf16)
+        variance = nn(square, mean_mat[pl.ds(0, channels), pl.ds(0, channels)])
         inv = lax.rsqrt(variance + norm_eps)
         unit_rows = centred * inv
         return unit_rows, inv, (unit_rows * gain_ref[...]).astype(bf16)
 
-    for index in range(4):
+    for index in (0, 1, 2, 3, 9):
         loads[index].wait()
 
     lanes = lax.broadcasted_iota(jnp.int32, (keys, channels), 1)
     subs = lax.broadcasted_iota(jnp.int32, (keys, channels), 0)
+    mean_mat[...] = jnp.zeros((2 * channels, 2 * channels), bf16)
+    mean_mat[pl.ds(0, channels), pl.ds(0, channels)] = jnp.full(
+        (channels, channels), 1.0 / channels, bf16
+    )
+    mean_mat[pl.ds(channels, channels), pl.ds(channels, channels)] = jnp.full(
+        (channels, channels), 1.0 / channels, bf16
+    )
+    kvw[:, :, pl.ds(2 * channels, channels)] = jnp.ones((windows, keys, channels), bf16)
     head_mask[...] = jnp.where(subs // qw == lanes // head_dim, 1.0, 0.0).astype(bf16)
 
     block = 256
+    group = 8
 
     def project(c, _):
         r = pl.multiple_of(c * block, block)
         unit_rows, inv, low = norm(state[pl.ds(r, block), :])
         unit[pl.ds(margin + r, block), :] = unit_rows
-        inverse[pl.ds(r, block), :] = jnp.broadcast_to(inv, (block, channels))
+        inverse[pl.ds(r, block), :] = inv
         normed[pl.ds(margin + r, block), :] = low
         qkv = nn(low, w3[...]).astype(bf16)
         queries[pl.ds(r, block), :] = qkv[:, :channels]
@@ -203,19 +225,20 @@
     tokens_up.start()
 
     spread[...] = jnp.zeros((2, full, channels), f32)
-    for slot in range(4):
+    for slot in range(2 * group):
         shift[slot, pl.ds(0, 2 * qw), :] = jnp.zeros((2 * qw, channels), f32)
         shift[slot, pl.ds(2 * qw + keys, 2 * qw), :] = jnp.zeros((2 * qw, channels), f32)
 
-    per_tile = rows // 128
+    for index in (11, 12, 13):
+        loads[index].wait()
     base = (me * toks).astype(f32)
     lower = base - toks
     sub_id = subs.astype(f32)
     lane_id = lanes.astype(f32)
     count_own = jnp.zeros((toks, 128), f32)
     count_low = jnp.zeros((toks, 128), f32)
-    for r in range(per_tile):
-        row = token_ref[pl.ds(me * per_tile + r, 1), :].astype(f32)
+    for r in range(tile):
+        row = token_ref[pl.ds(tile + r, 1), :].astype(f32)
         spot = jnp.broadcast_to(row, (128, 128))
         hit = jnp.where(spot - base == sub_id, 1.0, 0.0)
         count_own = count_own + hit
@@ -224,7 +247,7 @@
             hit = jnp.where(spot - lower == sub_id, 1.0, 0.0)
             count_low = count_low + hit
             sel_tlow[:, pl.ds(r * 128, 128)] = hit.astype(bf16)
-        column = spot.T - lower
+        column = (spot - lower).astype(bf16).T.astype(f32)
         sel_cat[pl.ds(r * 128, 128), pl.ds(0, 128)] = jnp.where(
             column == lane_id, 1.0, 0.0
         ).astype(bf16)
@@ -232,15 +255,13 @@
             column == lane_id + toks, 1.0, 0.0
         ).astype(bf16)
     has_above = jnp.where(me < A - 1, 1.0, 0.0)
-    above = jnp.minimum(me + 1, A - 1) * per_tile
     for r in range(2):
-        row = token_ref[pl.ds(above + r, 1), :].astype(f32)
+        row = token_ref[pl.ds(2 * tile + r, 1), :].astype(f32)
         spot = jnp.broadcast_to(row, (128, 128))
         count_own = count_own + jnp.where(spot - base == sub_id, has_above, 0.0)
     has_below = jnp.where(me > 0, 1.0, 0.0)
-    below = jnp.maximum(me - 1, 0) * per_tile
-    for r in range(per_tile):
-        row = token_ref[pl.ds(below + r, 1), :].astype(f32)
+    for r in range(tile):
+        row = token_ref[pl.ds(r, 1), :].astype(f32)
         spot = jnp.broadcast_to(row, (128, 128))
         count_low = count_low + jnp.where(spot - lower == sub_id, has_below, 0.0)
 
@@ -277,20 +298,22 @@
         q = spread_heads(queries[pl.ds(q0, qw), :])
         s = nt(q, k) * factor + bias[w]
         e = jnp.exp(s - jnp.max(s, axis=-1, keepdims=True))
-        p = (e / jnp.sum(e, axis=-1, keepdims=True)).astype(bf16)
-        probs[w] = p
-        attended[pl.ds(q0, qw), :] = gather_heads(nn(p, v)).astype(bf16)
-
-    near = (margin + qw - 1) // qw
+        mixed = nn(e.astype(bf16), kvw[w, :, pl.ds(channels, 2 * channels)])
+        scale = 1.0 / mixed[:, channels:]
+        probs[w] = (e * scale).astype(bf16)
+        attended[pl.ds(q0, qw), :] = gather_heads(mixed[:, :channels] * scale).astype(bf16)
+
+    near = group // 2
     loads[4].wait()
-
-    def forward_pair(i, _):
-        for k in range(2):
-            forward(lax.rem(2 * i + k + near, windows))
+    loads[10].wait()
+
+    def forward_group(i, _):
+        for k in range(group):
+            forward(lax.rem(group * i + k + near, windows))
         return 0
 
-    inner = (windows - 2 * near) // 2
-    lax.fori_loop(0, inner, forward_pair, 0)
+    inner = windows // group - 1
+    lax.fori_loop(0, inner, forward_group, 0)
 
     halo_left.wait_recv()
     halo_right.wait_recv()
@@ -299,14 +322,14 @@
         at = 0 if side == 0 else margin + rows
         keep = jnp.where(there, 1.0, 0.0)
         x = jnp.where(jnp.full((margin, channels), keep) > 0.0, halo[side].astype(f32), 0.0)
-        unit_rows, _, low = norm(x)
+        unit_rows, _, low = norm(x.astype(bf16))
         unit[pl.ds(at, margin), :] = unit_rows
         normed[pl.ds(at, margin), :] = low
         kv = nn(low, w3[:, channels:]).astype(bf16).astype(f32)
         kvf[0, pl.ds(at, margin), :] = kv[:, :channels]
         kvf[1, pl.ds(at, margin), :] = kv[:, channels:]
 
-    lax.fori_loop(inner, windows // 2, forward_pair, 0)
+    lax.fori_loop(inner, inner + 1, forward_group, 0)
 
     tokens_up.wait_recv()
     tokens_back[pl.ds(0, toks), :] = (ctok_low[...].astype(f32) * inverse_low).astype(bf16)
@@ -328,7 +351,11 @@
         active[here, :] = back
         sback = (cots[here, :].astype(f32) + nt(back, wt[...])).astype(bf16)
         state_back[here, :] = sback
-        attended_back[here, :] = nt(sback, wo[...]).astype(bf16)
+        aback = nt(sback, wo[...]).astype(bf16)
+        attended_back[here, pl.ds(0, channels)] = aback
+        attended_back[here, pl.ds(channels, channels)] = (
+            -aback.astype(f32) * attended[here, :].astype(f32)
+        ).astype(bf16)
 
     token_part(0)
     low_part[...] = nn(sel_tlow[...], silu[pl.ds(0, 256), :]).astype(bf16)
@@ -411,11 +438,11 @@
         kv = kvw[w]
         q0 = pl.multiple_of(w * qw, qw)
         q = spread_heads(queries[pl.ds(q0, qw), :])
-        da = spread_heads(attended_back[pl.ds(q0, qw), :])
+        da = spread_heads(attended_back[pl.ds(q0, qw), pl.ds(0, channels)])
+        delta = spread_heads(attended_back[pl.ds(q0, qw), pl.ds(channels, channels)])
         p = probs[w]
-        pf = p.astype(f32)
-        weighted = pf * nt(da, kv[:, channels:])
-        ds = (weighted - pf * jnp.sum(weighted, axis=-1, keepdims=True)).astype(bf16)
+        centred = nt(jnp.concatenate([da, delta], axis=1), kv[:, channels:])
+        ds = (p.astype(f32) * centred).astype(bf16)
         dq = gather_heads(nn(ds, kv[:, :channels]))
         query_back[pl.ds(q0, qw), :] = (dq * factor).astype(bf16)
         to = pl.ds(pl.multiple_of(base_atom - first_atom + margin, 16), span)
@@ -424,15 +451,15 @@
             moved = shift[2 * slot + part, pl.ds(2 * qw - off, span), :]
             spread[part, to, :] = spread[part, to, :] + moved
 
-    def backward_pair(i, _):
-        for k in range(2):
-            backward(2 * i + k, k)
+    def backward_group(i, _):
+        for k in range(group):
+            backward(group * i + k, k)
         return 0
 
-    lax.fori_loop(0, windows // 4, backward_pair, 0)
+    lax.fori_loop(0, windows // group // 2, backward_group, 0)
     scattered(e_src, e_rx1, e_sum, e_rx2, 4)
     exchange(e_sum, e_rx2, 5)
-    lax.fori_loop(windows // 4, windows // 2, backward_pair, 0)
+    lax.fori_loop(windows // group // 2, windows // group, backward_group, 0)
     exchanged(e_rx2, e_fin, 5)
     gather(e_fin, 6)
 
@@ -473,14 +500,13 @@
             nb = nb + extra
         ub = nb * gain_ref[...]
         un = unit[there, :]
+        means = nn(jnp.concatenate([ub, ub * un], axis=1).astype(bf16), mean_mat[...])
         grad_out[here, :] = state_back[here, :].astype(f32) + inverse[here, :] * (
-            ub
-            - jnp.mean(ub, axis=-1, keepdims=True)
-            - un * jnp.mean(ub * un, axis=-1, keepdims=True)
+            ub - means[:, :channels] - un * means[:, channels:]
         )
 
-    for r in range(0, rows - 2 * margin, 216):
-        norm_back(margin + r, min(216, rows - 2 * margin - r), None)
+    for r in range(0, rows - 2 * margin, 288):
+        norm_back(margin + r, min(288, rows - 2 * margin - r), None)
     back_left.wait_recv()
     back_right.wait_recv()
     norm_back(0, margin, nback_recv[0].astype(f32))
@@ -511,6 +537,85 @@
     ):
         wait_bytes(ref.at[pl.ds(0, count - 1)], send_sem.at[index])
     for copy in (out_state, out_rows, out_grad, out_early, out_late):
+        copy.wait()
+
+
+def finish(
+    scale,
+    state_hbm,
+    rows_hbm,
+    grad_hbm,
+    late_hbm,
+    early_hbm,
+    state_out,
+    rows_out,
+    grad_out,
+    gain_out,
+    query_out,
+    key_out,
+    value_out,
+    output_out,
+    token_out,
+    grad,
+    state,
+    token_rows,
+    late,
+    early,
+    gain,
+    square,
+    token,
+    in_sem,
+    out_sem,
+):
+    A, fold, wide = early.shape
+    half = fold // 2
+    channels = A * half
+    width = token.shape[1]
+    get_late = pltpu.make_async_copy(late_hbm, late, in_sem.at[0])
+    get_early = pltpu.make_async_copy(early_hbm, early, in_sem.at[1])
+    get_early.start()
+    get_late.start()
+    gets = [
+        pltpu.make_async_copy(src, dst, in_sem.at[2 + index])
+        for index, (src, dst) in enumerate(
+            ((grad_hbm, grad), (state_hbm, state), (rows_hbm, token_rows))
+        )
+    ]
+    for get in gets:
+        get.start()
+    puts = []
+
+    def put(src, dst, index):
+        copy = pltpu.make_async_copy(src, dst, out_sem.at[index])
+        copy.start()
+        puts.append(copy)
+
+    for index, (src, dst) in enumerate(
+        ((grad, grad_out), (state, state_out), (token_rows, rows_out))
+    ):
+        gets[index].wait()
+        put(src, dst, index)
+    get_early.wait()
+    low = early[:, :half, :].astype(f32) * scale
+    high = early[:, half:, :].astype(f32) * scale
+    mid = width // 2
+    token[:, pl.ds(0, mid)] = low[..., :mid].reshape(channels, mid)
+    token[:, pl.ds(mid, mid)] = high[..., :mid].reshape(channels, mid)
+    put(token, token_out, 3)
+    square[3] = (low[..., mid:] + high[..., mid:]).reshape(channels, channels)
+    put(square.at[3], output_out, 4)
+    get_late.wait()
+    low = late[:, :half, :].astype(f32) * scale
+    high = late[:, half:, :].astype(f32) * scale
+    square[0] = low[..., :channels].reshape(channels, channels)
+    square[1] = high[..., :channels].reshape(channels, channels)
+    square[2] = low[..., channels:].reshape(channels, channels)
+    put(square.at[0], query_out, 5)
+    put(square.at[1], key_out, 6)
+    put(square.at[2], value_out, 7)
+    gain[...] = jnp.sum(high[..., channels:].reshape(channels, channels), axis=0, keepdims=True)
+    put(gain, gain_out, 8)
+    for copy in puts:
         copy.wait()
 
 
@@ -541,9 +646,7 @@
     half = channels // A
     early = width // 2 + channels
     late = 2 * channels
-    any_spec = pl.BlockSpec(memory_space=pl.ANY)
-    vmem = pl.BlockSpec(memory_space=pltpu.VMEM)
-    smem = pl.BlockSpec(memory_space=pltpu.SMEM)
+    any_spec = pl.BlockSpec(memory_space=pltpu.HBM)
     V = pltpu.VMEM
     DMA = pltpu.SemaphoreType.DMA
     outs = pl.pallas_call(
@@ -555,12 +658,12 @@
             jax.ShapeDtypeStruct((A, fold, late), bf16),
             jax.ShapeDtypeStruct((A, fold, early), bf16),
         ),
-        in_specs=[any_spec, vmem]
-        + [any_spec] * 6
-        + [smem, vmem]
-        + [any_spec] * 2,
+        in_specs=[any_spec] * 12,
         out_specs=(any_spec,) * 5,
         scratch_shapes=[
+            V((1, channels), f32),
+            pltpu.SMEM((windows,), jnp.int32),
+            V((3 * rows // 128, 128), jnp.int32),
             V((rows, channels), bf16),
             V((channels, 3 * channels), bf16),
             V((channels, channels), bf16),
@@ -575,7 +678,7 @@
             V((full, channels), bf16),
             V((rows, channels), bf16),
             V((2, full, channels), f32),
-            V((windows, keys, 2 * channels), bf16),
+            V((windows, keys, 3 * channels), bf16),
             V((windows, heads * qw, keys), bf16),
             V((rows, channels), bf16),
             V((rows, channels), bf16),
@@ -587,11 +690,11 @@
             V((rows, width), bf16),
             V((rows, width), bf16),
             V((rows, channels), bf16),
-            V((rows, channels), bf16),
+            V((rows, 2 * channels), bf16),
             V((toks, width), bf16),
             V((toks, width), bf16),
             V((toks, width), bf16),
-            V((4, keys + 4 * qw, channels), f32),
+            V((16, keys + 4 * qw, channels), f32),
             V((2, full, channels), f32),
             V((rows, channels), bf16),
             V((full, 2 * channels), bf16),
@@ -610,13 +713,14 @@
             V((B, fold, late), bf16),
             V((A, fold, late), bf16),
             V((keys, channels), bf16),
-            DMA((9,)),
+            V((2 * channels, 2 * channels), bf16),
+            DMA((14,)),
             DMA((5,)),
             DMA((12,)),
             DMA((12,)),
         ],
         compiler_params=pltpu.CompilerParams(
-            collective_id=0, has_side_effects=True, vmem_limit_bytes=48 * 1024 * 1024
+            collective_id=0, has_side_effects=True, vmem_limit_bytes=62 * 1024 * 1024
         ),
         name="atom_block",
     )(
@@ -633,32 +737,39 @@
         cotangent_state,
         cotangent_tokens,
     )
-    state_out, token_rows, grad_state, late_sum, early_sum = outs
     rescale = 1.0 / math.sqrt(B * A * rows)
-    late_sum = late_sum.astype(f32) * rescale
-    early_sum = early_sum.astype(f32) * rescale
-    square = (channels, channels)
-    grad_query = late_sum[:, :half, :channels].reshape(square)
-    grad_key = late_sum[:, half:, :channels].reshape(square)
-    grad_value = late_sum[:, :half, channels:].reshape(square)
-    grad_gain = jnp.sum(late_sum[:, half:, channels:], axis=(0, 1))
-    grad_token = jnp.concatenate(
-        [early_sum[:, :half, : width // 2], early_sum[:, half:, : width // 2]], axis=-1
-    ).reshape(channels, width)
-    grad_output = (
-        early_sum[:, :half, width // 2 :] + early_sum[:, half:, width // 2 :]
-    ).reshape(square)
-    return (
-        state_out,
-        token_rows,
-        grad_state,
-        grad_gain,
-        grad_query,
-        grad_key,
-        grad_value,
-        grad_output,
-        grad_token,
-    )
+    square = jax.ShapeDtypeStruct((channels, channels), f32)
+    done = pl.pallas_call(
+        functools.partial(finish, rescale),
+        out_shape=(
+            jax.ShapeDtypeStruct((1, rows, channels), bf16),
+            jax.ShapeDtypeStruct((1, toks, width), bf16),
+            jax.ShapeDtypeStruct((1, rows, channels), f32),
+            jax.ShapeDtypeStruct((1, channels), f32),
+            square,
+            square,
+            square,
+            square,
+            jax.ShapeDtypeStruct((channels, width), f32),
+        ),
+        in_specs=[any_spec] * 5,
+        out_specs=(any_spec,) * 9,
+        scratch_shapes=[
+            V((1, rows, channels), f32),
+            V((1, rows, channels), bf16),
+            V((1, toks, width), bf16),
+            V((A, fold, late), bf16),
+            V((A, fold, early), bf16),
+            V((1, channels), f32),
+            V((4, channels, channels), f32),
+            V((channels, width), f32),
+            DMA((5,)),
+            DMA((9,)),
+        ],
+        compiler_params=pltpu.CompilerParams(vmem_limit_bytes=62 * 1024 * 1024),
+        name="finish",
+    )(*outs)
+    return done[:3] + (done[3].reshape(channels),) + done[4:]
 
 
 def solution(mesh):

time: 81.2 us -> 63.7 us (0.78)
  local copies, waits for them, and re-layouts: 12.7 us -> 0 us
  other arithmetic: 2.69 us -> 0 us
  Pallas kernels: 64.6 us -> 62.9 us
    unnamed x27 -> x0, local copies, waits for them, and re-layouts: 12.7 us -> none
    pallas_call x1, Pallas kernels: 64.6 us -> 60.4 us  [on_device(): pl.pallas_call(functools.partial(kernel, sizes), out_shape=(jax.ShapeDtyp...]
    reshape x3 -> x0, other arithmetic: 2.62 us -> none  [the longest x1 1.19 us: on_device(): grad_value = late_sum[:, :half, channels:].reshape(square)]
    pallas_call x0 -> x1, Pallas kernels: none -> 2.46 us  [on_device(): pl.pallas_call(functools.partial(finish, rescale), out_shape=(jax.ShapeDt...]
where the time goes in v2:
time: 63.7 us; the launch traced here: 63.6 us
  Pallas kernels  62.9 us (99%)
  between operations  0.65 us (1%)
    pallas_call x1, Pallas kernels, on_device(): pl.pallas_call(functools.partial(kernel, sizes), out_shape=(jax.ShapeDtyp...  60.4 us
    pallas_call x1, Pallas kernels, on_device(): pl.pallas_call(functools.partial(finish, rescale), out_shape=(jax.ShapeDt...  2.46 us

profile of v2, /device:TPU:1, one launch (start us, length us, event | category | flops | bytes accessed | tf_op | source)
XLA Modules:
  0.0 63.6 jit_solution(4479661495474783060)
XLA Ops:
  0.6 60.4 %atom_block.1 = (bf16[1,1024,128]{2,1,0:T(8,128)(2,1)}, bf16[1,128,768]{2,1,0:T(8,128)(2,1)}, f32[1,1024,128]{2,1,0:T(8,128)}, bf16[16,16,256]{2,1,0:T(8,128)(2,1)}, bf16[16,16,512]{2,1,0:T(8,128)(2,1)}) custom-call(bf16[1,1024,128]{2,1,0:T(8,128)(2,1)} %state_hbm.1, f32[1,128]{1,0:T(1,128)} %bitcast.6, bf16[128,128]{1,0:T(8,128)(2,1)} %wq_hbm.1, ...), custom_call_target="tpu_custom_call" | custom-call | tf_op jit(solution)/shard_map/atom_block/pallas_call | solution.py:652
  61.1 2.5 %finish.1 = (bf16[1,1024,128]{2,1,0:T(8,128)(2,1)}, bf16[1,128,768]{2,1,0:T(8,128)(2,1)}, f32[1,1024,128]{2,1,0:T(8,128)}, f32[1,128]{1,0:T(1,128)}, f32[128,128...) custom-call(bf16[1,1024,128]{2,1,0:T(8,128)(2,1)} %get-tuple-element.23.state, ...), custom_call_target="tpu_custom_call" | custom-call | tf_op jit(solution)/shard_map/finish/pallas_call | solution.py:742

commit v3 on v2

--- a/solution.py
+++ b/solution.py
@@ -103,14 +103,15 @@
     send_sem,
     recv_sem,
 ):
-    A, B, rows, channels, windows, heads, qw, keys, toks, width = sizes
+    A, B, planes, rows, channels, windows, heads, qw, keys, toks, width = sizes
     margin = keys // 2 + qw // 2
     full = rows + 2 * margin
     span = keys + 2 * qw
     head_dim = channels // heads
     factor = head_dim ** (-0.5)
-    fold = 2 * channels // A
-    half = channels // A
+    G = A * planes
+    Z = B // planes
+    half = 2 * channels // G
     me = lax.axis_index("atom")
     smp = lax.axis_index("sample")
     left = {"atom": lax.rem(me + A - 1, A)}
@@ -141,20 +142,29 @@
     ]
     barrier = pltpu.get_barrier_semaphore()
 
+    rank = lax.div(smp, Z) * A + me
+    depth = lax.rem(smp, Z)
+
+    def plane_peer(p):
+        return {"sample": lax.div(p, A) * Z + depth, "atom": lax.rem(p, A)}
+
+    def line_peer(q):
+        return {"sample": lax.div(smp, Z) * Z + q}
+
     def greet(d, _):
         pl.semaphore_signal(
-            barrier, inc=1, device_id={"atom": lax.rem(me + d, A)}, device_id_type=MESH
+            barrier, inc=1, device_id=plane_peer(lax.rem(rank + d, G)), device_id_type=MESH
         )
         return 0
 
-    def greet_sample(d, _):
+    def greet_line(d, _):
         pl.semaphore_signal(
-            barrier, inc=1, device_id={"sample": lax.rem(smp + d, B)}, device_id_type=MESH
+            barrier, inc=1, device_id=line_peer(lax.rem(depth + d, Z)), device_id_type=MESH
         )
         return 0
 
-    lax.fori_loop(1, A, greet, 0)
-    lax.fori_loop(1, B, greet_sample, 0)
+    lax.fori_loop(1, G, greet, 0)
+    lax.fori_loop(1, Z, greet_line, 0)
 
     for copy in loads:
         copy.start()
@@ -213,7 +223,7 @@
 
     lax.fori_loop(0, rows // block, project, 0)
 
-    pl.semaphore_wait(barrier, A + B - 2)
+    pl.semaphore_wait(barrier, G + Z - 2)
 
     halo_left = send(
         state_hbm.at[0, pl.ds(rows - margin, margin), :], halo.at[0], 0, right
@@ -369,66 +379,64 @@
     out_state = store(state_out, state_out_hbm.at[0], 0)
     out_state.start()
 
-    def folded(x):
-        x = x.reshape(A, half, x.shape[-1])
-        mid = x.shape[-1] // 2
-        return jnp.concatenate([x[..., :mid], x[..., mid:]], axis=1)
-
     def stacked(x, y):
         return jnp.concatenate(
-            [x.reshape(A, half, channels), y.reshape(A, half, channels)], axis=1
-        )
+            [x.reshape(G // 2, half, channels), y.reshape(G // 2, half, channels)], axis=1
+        ).astype(bf16)
+
+    first, second = pl.ds(0, G // 2), pl.ds(G // 2, G // 2)
 
     token_sum = tn(state_out[...], active[...])
-    e_src[:, :, pl.ds(0, width // 2)] = folded(token_sum).astype(bf16)
+    pieces = [token_sum[:, c : c + channels] for c in range(0, width, channels)]
     output_sum = tn(attended[...], state_back[...])
     output_high = output_sum.astype(bf16).astype(f32)
-    e_src[:, :, pl.ds(width // 2, channels)] = stacked(
-        output_high, output_sum - output_high
-    ).astype(bf16)
+    e_src[first, :, pl.ds(0, channels)] = stacked(pieces[0], pieces[1])
+    e_src[first, :, pl.ds(channels, channels)] = stacked(pieces[2], pieces[3])
+    e_src[second, :, pl.ds(0, channels)] = stacked(pieces[4], pieces[5])
+    e_src[second, :, pl.ds(channels, channels)] = stacked(output_high, output_sum - output_high)
 
     def scatter(src, rx, index):
         def one(d, _):
-            peer = lax.rem(me + d, A)
-            send(src.at[peer], rx.at[d], index, {"atom": peer}).start()
+            peer = lax.rem(rank + d, G)
+            send(src.at[peer], rx.at[d], index, plane_peer(peer)).start()
             return 0
 
-        lax.fori_loop(1, A, one, 0)
+        lax.fori_loop(1, G, one, 0)
 
     def scattered(src, rx, part, rx2, index):
-        wait_bytes(rx.at[pl.ds(1, A - 1)], recv_sem.at[index])
-        total = src[me].astype(f32)
-        for d in range(1, A):
+        wait_bytes(rx.at[pl.ds(1, G - 1)], recv_sem.at[index])
+        total = src[rank].astype(f32)
+        for d in range(1, G):
             total = total + rx[d].astype(f32)
         low = total.astype(bf16)
         part[...] = low
-        rx2[smp] = low
+        rx2[depth] = low
 
     def exchange(part, rx2, index):
         def one(d, _):
-            peer = lax.rem(smp + d, B)
-            send(part, rx2.at[smp], index, {"sample": peer}).start()
+            peer = lax.rem(depth + d, Z)
+            send(part, rx2.at[depth], index, line_peer(peer)).start()
             return 0
 
-        lax.fori_loop(1, B, one, 0)
+        lax.fori_loop(1, Z, one, 0)
 
     def exchanged(rx2, fin, index):
-        wait_bytes(rx2.at[pl.ds(0, B - 1)], recv_sem.at[index])
+        wait_bytes(rx2.at[pl.ds(0, Z - 1)], recv_sem.at[index])
         total = rx2[0].astype(f32)
-        for d in range(1, B):
+        for d in range(1, Z):
             total = total + rx2[d].astype(f32)
-        fin[me] = total.astype(bf16)
+        fin[rank] = total.astype(bf16)
 
     def gather(fin, index):
         def one(d, _):
-            peer = lax.rem(me + d, A)
-            send(fin.at[me], fin.at[me], index, {"atom": peer}).start()
+            peer = lax.rem(rank + d, G)
+            send(fin.at[rank], fin.at[rank], index, plane_peer(peer)).start()
             return 0
 
-        lax.fori_loop(1, A, one, 0)
+        lax.fori_loop(1, G, one, 0)
 
     def gathered(fin, index):
-        wait_bytes(fin.at[pl.ds(0, A - 1)], recv_sem.at[index])
+        wait_bytes(fin.at[pl.ds(0, G - 1)], recv_sem.at[index])
 
     scatter(e_src, e_rx1, 4)
 
@@ -456,15 +464,26 @@
             backward(group * i + k, k)
         return 0
 
-    lax.fori_loop(0, windows // group // 2, backward_group, 0)
+    lax.fori_loop(0, windows // group, backward_group, 0)
     scattered(e_src, e_rx1, e_sum, e_rx2, 4)
     exchange(e_sum, e_rx2, 5)
-    lax.fori_loop(windows // group // 2, windows // group, backward_group, 0)
-    exchanged(e_rx2, e_fin, 5)
-    gather(e_fin, 6)
-
+
+    own = pl.ds(margin, rows)
     spread_low[:, pl.ds(0, channels)] = spread[0].astype(bf16)
     spread_low[:, pl.ds(channels, channels)] = spread[1].astype(bf16)
+    query_sum = tn(normed[own, :], query_back[...])
+    pair_sum = tn(normed[...], spread_low[...])
+    weighted = (
+        w3[:, :channels].astype(f32) * query_sum
+        + w3[:, channels : 2 * channels].astype(f32) * pair_sum[:, :channels]
+        + w3[:, 2 * channels :].astype(f32) * pair_sum[:, channels:]
+    )
+    gain_part = jnp.sum(weighted.T.reshape(channels // 8, 8, channels), axis=0) / gain_ref[...]
+    gain_rows = jnp.concatenate([gain_part, jnp.zeros((channels - 8, channels), f32)], axis=0)
+    l_src[first] = stacked(query_sum, pair_sum[:, :channels])
+    l_src[second] = stacked(pair_sum[:, channels:], gain_rows)
+    scatter(l_src, l_rx1, 9)
+
     nback[...] = nt(spread_low[...], w3[:, channels:])
     nback_send[0] = nback[pl.ds(0, margin), :].astype(bf16)
     nback_send[1] = nback[pl.ds(margin + rows, margin), :].astype(bf16)
@@ -472,17 +491,7 @@
     back_right = send(nback_send.at[1], nback_recv.at[0], 8, right)
     back_left.start()
     back_right.start()
-    own = pl.ds(margin, rows)
     nback[own, :] = nback[own, :] + nt(query_back[...], w3[:, :channels])
-    query_sum = tn(normed[own, :], query_back[...])
-    pair_sum = tn(normed[...], spread_low[...])
-    gain_part = jnp.sum((unit[...] * nback[...]).reshape(full // 8, 8, channels), axis=0)
-    gain_rows = jnp.concatenate([gain_part, jnp.zeros((channels - 8, channels), f32)], axis=0)
-    l_src[:, :, pl.ds(0, channels)] = stacked(query_sum, pair_sum[:, :channels]).astype(bf16)
-    l_src[:, :, pl.ds(channels, channels)] = stacked(pair_sum[:, channels:], gain_rows).astype(
-        bf16
-    )
-    scatter(l_src, l_rx1, 9)
 
     part_down.wait_recv()
     own_part = nn(sel_t[...], silu[...])
@@ -507,20 +516,21 @@
 
     for r in range(0, rows - 2 * margin, 288):
         norm_back(margin + r, min(288, rows - 2 * margin - r), None)
+    scattered(l_src, l_rx1, l_sum, l_rx2, 9)
+    exchange(l_sum, l_rx2, 10)
+    exchanged(e_rx2, e_fin, 5)
+    gather(e_fin, 6)
     back_left.wait_recv()
     back_right.wait_recv()
     norm_back(0, margin, nback_recv[0].astype(f32))
     norm_back(rows - margin, margin, nback_recv[1].astype(f32))
     out_grad = store(grad_out, grad_out_hbm.at[0], 2)
     out_grad.start()
-
-    scattered(l_src, l_rx1, l_sum, l_rx2, 9)
-    exchange(l_sum, l_rx2, 10)
+    exchanged(l_rx2, l_fin, 10)
+    gather(l_fin, 11)
     gathered(e_fin, 6)
     out_early = store(e_fin, early_out_hbm, 3)
     out_early.start()
-    exchanged(l_rx2, l_fin, 10)
-    gather(l_fin, 11)
     gathered(l_fin, 11)
     out_late = store(l_fin, late_out_hbm, 4)
     out_late.start()
@@ -528,12 +538,12 @@
     for copy in (halo_left, halo_right, tokens_up, part_down, back_left, back_right):
         copy.wait_send()
     for index, ref, count in (
-        (4, e_rx1, A),
-        (5, e_rx2, B),
-        (6, e_fin, A),
-        (9, l_rx1, A),
-        (10, l_rx2, B),
-        (11, l_fin, A),
+        (4, e_rx1, G),
+        (5, e_rx2, Z),
+        (6, e_fin, G),
+        (9, l_rx1, G),
+        (10, l_rx2, Z),
+        (11, l_fin, G),
     ):
         wait_bytes(ref.at[pl.ds(0, count - 1)], send_sem.at[index])
     for copy in (out_state, out_rows, out_grad, out_early, out_late):
@@ -567,10 +577,16 @@
     in_sem,
     out_sem,
 ):
-    A, fold, wide = early.shape
+    G, fold, _ = early.shape
     half = fold // 2
-    channels = A * half
-    width = token.shape[1]
+    channels = late.shape[2]
+    first, second = slice(0, G // 2), slice(G // 2, G)
+    upper, lower = slice(0, half), slice(half, fold)
+
+    def matrix(ref, part, piece, column):
+        chunk = ref[part, piece, column * channels : (column + 1) * channels]
+        return chunk.astype(f32).reshape(channels, channels) * scale
+
     get_late = pltpu.make_async_copy(late_hbm, late, in_sem.at[0])
     get_early = pltpu.make_async_copy(early_hbm, early, in_sem.at[1])
     get_early.start()
@@ -596,24 +612,22 @@
         gets[index].wait()
         put(src, dst, index)
     get_early.wait()
-    low = early[:, :half, :].astype(f32) * scale
-    high = early[:, half:, :].astype(f32) * scale
-    mid = width // 2
-    token[:, pl.ds(0, mid)] = low[..., :mid].reshape(channels, mid)
-    token[:, pl.ds(mid, mid)] = high[..., :mid].reshape(channels, mid)
+    places = ((first, 0), (first, 1), (second, 0))
+    for index, (part, column) in enumerate(places):
+        for k, piece in enumerate((upper, lower)):
+            to = pl.ds((2 * index + k) * channels, channels)
+            token[:, to] = matrix(early, part, piece, column)
     put(token, token_out, 3)
-    square[3] = (low[..., mid:] + high[..., mid:]).reshape(channels, channels)
+    square[3] = matrix(early, second, upper, 1) + matrix(early, second, lower, 1)
     put(square.at[3], output_out, 4)
     get_late.wait()
-    low = late[:, :half, :].astype(f32) * scale
-    high = late[:, half:, :].astype(f32) * scale
-    square[0] = low[..., :channels].reshape(channels, channels)
-    square[1] = high[..., :channels].reshape(channels, channels)
-    square[2] = low[..., channels:].reshape(channels, channels)
+    square[0] = matrix(late, first, upper, 0)
+    square[1] = matrix(late, first, lower, 0)
+    square[2] = matrix(late, second, upper, 0)
     put(square.at[0], query_out, 5)
     put(square.at[1], key_out, 6)
     put(square.at[2], value_out, 7)
-    gain[...] = jnp.sum(high[..., channels:].reshape(channels, channels), axis=0, keepdims=True)
+    gain[...] = jnp.sum(matrix(late, second, lower, 0), axis=0, keepdims=True)
     put(gain, gain_out, 8)
     for copy in puts:
         copy.wait()
@@ -638,14 +652,16 @@
     _, rows, channels = atom_state.shape
     windows, heads, qw, keys = pair_bias.shape
     toks, width = cotangent_tokens.shape[1:]
-    sizes = (A, B, rows, channels, windows, heads, qw, keys, toks, width)
+    planes = 2
+    sizes = (A, B, planes, rows, channels, windows, heads, qw, keys, toks, width)
     margin = keys // 2 + qw // 2
     full = rows + 2 * margin
     span = keys + 2 * qw
-    fold = 2 * channels // A
-    half = channels // A
-    early = width // 2 + channels
-    late = 2 * channels
+    G = A * planes
+    Z = B // planes
+    fold = 4 * channels // G
+    early = 2 * channels
+    late = channels
     any_spec = pl.BlockSpec(memory_space=pltpu.HBM)
     V = pltpu.VMEM
     DMA = pltpu.SemaphoreType.DMA
@@ -655,8 +671,8 @@
             jax.ShapeDtypeStruct((1, rows, channels), bf16),
             jax.ShapeDtypeStruct((1, toks, width), bf16),
             jax.ShapeDtypeStruct((1, rows, channels), f32),
-            jax.ShapeDtypeStruct((A, fold, late), bf16),
-            jax.ShapeDtypeStruct((A, fold, early), bf16),
+            jax.ShapeDtypeStruct((G, fold, late), bf16),
+            jax.ShapeDtypeStruct((G, fold, early), bf16),
         ),
         in_specs=[any_spec] * 12,
         out_specs=(any_spec,) * 5,
@@ -702,16 +718,16 @@
             V((2, margin, channels), bf16),
             V((2, margin, channels), bf16),
             V((rows, channels), f32),
-            V((A, fold, early), bf16),
-            V((A, fold, early), bf16),
+            V((G, fold, early), bf16),
+            V((G, fold, early), bf16),
             V((fold, early), bf16),
-            V((B, fold, early), bf16),
-            V((A, fold, early), bf16),
-            V((A, fold, late), bf16),
-            V((A, fold, late), bf16),
+            V((Z, fold, early), bf16),
+            V((G, fold, early), bf16),
+            V((G, fold, late), bf16),
+            V((G, fold, late), bf16),
             V((fold, late), bf16),
-            V((B, fold, late), bf16),
-            V((A, fold, late), bf16),
+            V((Z, fold, late), bf16),
+            V((G, fold, late), bf16),
             V((keys, channels), bf16),
             V((2 * channels, 2 * channels), bf16),
             DMA((14,)),
@@ -758,8 +774,8 @@
             V((1, rows, channels), f32),
             V((1, rows, channels), bf16),
             V((1, toks, width), bf16),
-            V((A, fold, late), bf16),
-            V((A, fold, early), bf16),
+            V((G, fold, late), bf16),
+            V((G, fold, early), bf16),
             V((1, channels), f32),
             V((4, channels, channels), f32),
             V((channels, width), f32),

time: 63.7 us -> 51 us (0.80)
  Pallas kernels: 62.9 us -> 50.2 us
    pallas_call x1, Pallas kernels: 60.4 us -> 47.7 us  [on_device(): pl.pallas_call(functools.partial(kernel, sizes), out_shape=(jax.ShapeDtyp...]
where the time goes in v3:
time: 51 us; the launch traced here: 50.8 us
  Pallas kernels  50.2 us (98%)
  between operations  0.65 us (1%)
    pallas_call x1, Pallas kernels, on_device(): pl.pallas_call(functools.partial(kernel, sizes), out_shape=(jax.ShapeDtyp...  47.7 us
    pallas_call x1, Pallas kernels, on_device(): pl.pallas_call(functools.partial(finish, rescale), out_shape=(jax.ShapeDt...  2.46 us

profile of v3, /device:TPU:1, one launch (start us, length us, event | category | flops | bytes accessed | tf_op | source)
XLA Modules:
  0.0 50.8 jit_solution(6011967769178963387)
XLA Ops:
  0.6 47.7 %atom_block.1 = (bf16[1,1024,128]{2,1,0:T(8,128)(2,1)}, bf16[1,128,768]{2,1,0:T(8,128)(2,1)}, f32[1,1024,128]{2,1,0:T(8,128)}, bf16[32,16,128]{2,1,0:T(8,128)(2,1)}, bf16[32,16,256]{2,1,0:T(8,128)(2,1)}) custom-call(bf16[1,1024,128]{2,1,0:T(8,128)(2,1)} %state_hbm.1, f32[1,128]{1,0:T(1,128)} %bitcast.6, bf16[128,128]{1,0:T(8,128)(2,1)} %wq_hbm.1, ...), custom_call_target="tpu_custom_call" | custom-call | tf_op jit(solution)/shard_map/atom_block/pallas_call | solution.py:668
  48.4 2.5 %finish.1 = (bf16[1,1024,128]{2,1,0:T(8,128)(2,1)}, bf16[1,128,768]{2,1,0:T(8,128)(2,1)}, f32[1,1024,128]{2,1,0:T(8,128)}, f32[1,128]{1,0:T(1,128)}, f32[128,128...) custom-call(bf16[1,1024,128]{2,1,0:T(8,128)(2,1)} %get-tuple-element.23.state, ...), custom_call_target="tpu_custom_call" | custom-call | tf_op jit(solution)/shard_map/finish/pallas_call | solution.py:758

commit v4 on v3

--- a/solution.py
+++ b/solution.py
@@ -203,7 +203,6 @@
     mean_mat[pl.ds(channels, channels), pl.ds(channels, channels)] = jnp.full(
         (channels, channels), 1.0 / channels, bf16
     )
-    kvw[:, :, pl.ds(2 * channels, channels)] = jnp.ones((windows, keys, channels), bf16)
     head_mask[...] = jnp.where(subs // qw == lanes // head_dim, 1.0, 0.0).astype(bf16)
 
     block = 256
@@ -298,28 +297,35 @@
             out = jnp.where(lane >= h * head_dim, x[h * qw : (h + 1) * qw], out)
         return out
 
-    def forward(w):
-        place = jnp.clip(start_ref[w] - first_atom + margin, 0, full - keys)
-        k = kvf[0, pl.ds(place, keys), :].astype(bf16)
-        v = kvf[1, pl.ds(place, keys), :].astype(bf16)
-        kvw[w, :, pl.ds(0, channels)] = k
-        kvw[w, :, pl.ds(channels, channels)] = v
-        q0 = pl.multiple_of(w * qw, qw)
-        q = spread_heads(queries[pl.ds(q0, qw), :])
-        s = nt(q, k) * factor + bias[w]
-        e = jnp.exp(s - jnp.max(s, axis=-1, keepdims=True))
-        mixed = nn(e.astype(bf16), kvw[w, :, pl.ds(channels, 2 * channels)])
-        scale = 1.0 / mixed[:, channels:]
-        probs[w] = (e * scale).astype(bf16)
-        attended[pl.ds(q0, qw), :] = gather_heads(mixed[:, :channels] * scale).astype(bf16)
+    def forward(ws):
+        queries_of, keys_of, values_of, scores, weights, mixes = [], [], [], [], [], []
+        for w in ws:
+            place = jnp.clip(start_ref[w] - first_atom + margin, 0, full - keys)
+            keys_of.append(kvf[0, pl.ds(place, keys), :].astype(bf16))
+            values_of.append(kvf[1, pl.ds(place, keys), :].astype(bf16))
+            q0 = pl.multiple_of(w * qw, qw)
+            queries_of.append(spread_heads(queries[pl.ds(q0, qw), :]))
+        for w, q, k in zip(ws, queries_of, keys_of):
+            scores.append(nt(q, k) * factor + bias[w])
+        for s in scores:
+            weights.append(jnp.exp(s - jnp.max(s, axis=-1, keepdims=True)))
+        ones = jnp.ones((keys, channels), bf16)
+        for e, v in zip(weights, values_of):
+            mixes.append(nn(e.astype(bf16), jnp.concatenate([v, ones], axis=1)))
+        for w, e, mixed, k, v in zip(ws, weights, mixes, keys_of, values_of):
+            scale = 1.0 / mixed[:, channels:]
+            probs[w] = (e * scale).astype(bf16)
+            q0 = pl.multiple_of(w * qw, qw)
+            attended[pl.ds(q0, qw), :] = gather_heads(mixed[:, :channels] * scale).astype(bf16)
+            kvw[w, :, pl.ds(0, channels)] = k
+            kvw[w, :, pl.ds(channels, channels)] = v
 
     near = group // 2
     loads[4].wait()
     loads[10].wait()
 
     def forward_group(i, _):
-        for k in range(group):
-            forward(lax.rem(group * i + k + near, windows))
+        forward([lax.rem(group * i + j + near, windows) for j in range(group)])
         return 0
 
     inner = windows // group - 1
@@ -440,28 +446,42 @@
 
     scatter(e_src, e_rx1, 4)
 
-    def backward(w, slot):
-        base_atom = jnp.clip(first_atom + w * qw - margin, 0, last_base)
-        off = jnp.clip(start_ref[w] - base_atom, 0, 2 * qw)
-        kv = kvw[w]
-        q0 = pl.multiple_of(w * qw, qw)
-        q = spread_heads(queries[pl.ds(q0, qw), :])
-        da = spread_heads(attended_back[pl.ds(q0, qw), pl.ds(0, channels)])
-        delta = spread_heads(attended_back[pl.ds(q0, qw), pl.ds(channels, channels)])
-        p = probs[w]
-        centred = nt(jnp.concatenate([da, delta], axis=1), kv[:, channels:])
-        ds = (p.astype(f32) * centred).astype(bf16)
-        dq = gather_heads(nn(ds, kv[:, :channels]))
-        query_back[pl.ds(q0, qw), :] = (dq * factor).astype(bf16)
-        to = pl.ds(pl.multiple_of(base_atom - first_atom + margin, 16), span)
-        for part, rows_back in enumerate((tn(ds, q) * factor, tn(p, da))):
-            shift[2 * slot + part, pl.ds(2 * qw, keys), :] = rows_back
-            moved = shift[2 * slot + part, pl.ds(2 * qw - off, span), :]
-            spread[part, to, :] = spread[part, to, :] + moved
+    def backward(ws, slots):
+        state_of = []
+        for w in ws:
+            kv = kvw[w]
+            q0 = pl.multiple_of(w * qw, qw)
+            q = spread_heads(queries[pl.ds(q0, qw), :])
+            da = spread_heads(attended_back[pl.ds(q0, qw), pl.ds(0, channels)])
+            delta = spread_heads(attended_back[pl.ds(q0, qw), pl.ds(channels, channels)])
+            state_of.append((kv, q0, q, da, delta, probs[w]))
+        ones = jnp.ones((keys, channels), bf16)
+        centred = [
+            nt(
+                jnp.concatenate([da, delta], axis=1),
+                jnp.concatenate([kv[:, channels:], ones], axis=1),
+            )
+            for kv, q0, q, da, delta, p in state_of
+        ]
+        lows = [
+            (st[5].astype(f32) * c).astype(bf16) for st, c in zip(state_of, centred)
+        ]
+        for ds, (kv, q0, q, da, delta, p) in zip(lows, state_of):
+            dq = gather_heads(nn(ds, kv[:, :channels]))
+            query_back[pl.ds(q0, qw), :] = (dq * factor).astype(bf16)
+        for slot, ds, (kv, q0, q, da, delta, p) in zip(slots, lows, state_of):
+            shift[2 * slot, pl.ds(2 * qw, keys), :] = tn(ds, q) * factor
+            shift[2 * slot + 1, pl.ds(2 * qw, keys), :] = tn(p, da)
+        for w, slot in zip(ws, slots):
+            base_atom = jnp.clip(first_atom + w * qw - margin, 0, last_base)
+            off = jnp.clip(start_ref[w] - base_atom, 0, 2 * qw)
+            to = pl.ds(pl.multiple_of(base_atom - first_atom + margin, 16), span)
+            for part in range(2):
+                moved = shift[2 * slot + part, pl.ds(2 * qw - off, span), :]
+                spread[part, to, :] = spread[part, to, :] + moved
 
     def backward_group(i, _):
-        for k in range(group):
-            backward(group * i + k, k)
+        backward([group * i + j for j in range(group)], list(range(group)))
         return 0
 
     lax.fori_loop(0, windows // group, backward_group, 0)
@@ -694,7 +714,7 @@
             V((full, channels), bf16),
             V((rows, channels), bf16),
             V((2, full, channels), f32),
-            V((windows, keys, 3 * channels), bf16),
+            V((windows, keys, 2 * channels), bf16),
             V((windows, heads * qw, keys), bf16),
             V((rows, channels), bf16),
             V((rows, channels), bf16),

time: 51 us -> 47.1 us (0.924)
  Pallas kernels: 50.2 us -> 46.3 us
    pallas_call x1, Pallas kernels: 47.7 us -> 43.8 us  [on_device(): pl.pallas_call(functools.partial(kernel, sizes), out_shape=(jax.ShapeDtyp...]
where the time goes in v4:
time: 47.1 us; the launch traced here: 46.9 us
  Pallas kernels  46.3 us (98%)
  between operations  0.65 us (1%)
    pallas_call x1, Pallas kernels, on_device(): pl.pallas_call(functools.partial(kernel, sizes), out_shape=(jax.ShapeDtyp...  43.8 us
    pallas_call x1, Pallas kernels, on_device(): pl.pallas_call(functools.partial(finish, rescale), out_shape=(jax.ShapeDt...  2.46 us

profile of v4, /device:TPU:1, one launch (start us, length us, event | category | flops | bytes accessed | tf_op | source)
XLA Modules:
  0.0 46.9 jit_solution(17989534865550937824)
XLA Ops:
  0.6 43.8 %atom_block.1 = (bf16[1,1024,128]{2,1,0:T(8,128)(2,1)}, bf16[1,128,768]{2,1,0:T(8,128)(2,1)}, f32[1,1024,128]{2,1,0:T(8,128)}, bf16[32,16,128]{2,1,0:T(8,128)(2,1)}, bf16[32,16,256]{2,1,0:T(8,128)(2,1)}) custom-call(bf16[1,1024,128]{2,1,0:T(8,128)(2,1)} %state_hbm.1, f32[1,128]{1,0:T(1,128)} %bitcast.6, bf16[128,128]{1,0:T(8,128)(2,1)} %wq_hbm.1, ...), custom_call_target="tpu_custom_call" | custom-call | tf_op jit(solution)/shard_map/atom_block/pallas_call | solution.py:688
  44.5 2.5 %finish.1 = (bf16[1,1024,128]{2,1,0:T(8,128)(2,1)}, bf16[1,128,768]{2,1,0:T(8,128)(2,1)}, f32[1,1024,128]{2,1,0:T(8,128)}, f32[1,128]{1,0:T(1,128)}, f32[128,128...) custom-call(bf16[1,1024,128]{2,1,0:T(8,128)(2,1)} %get-tuple-element.23.state, ...), custom_call_target="tpu_custom_call" | custom-call | tf_op jit(solution)/shard_map/finish/pallas_call | solution.py:778

commit v5 on v4

--- a/solution.py
+++ b/solution.py
@@ -40,11 +40,15 @@
     token_hbm,
     cots_hbm,
     ctok_hbm,
-    state_out_hbm,
-    rows_out_hbm,
-    grad_out_hbm,
-    late_out_hbm,
-    early_out_hbm,
+    state_out_ref,
+    rows_out_ref,
+    grad_out_ref,
+    gain_out,
+    query_out,
+    key_out,
+    value_out,
+    output_out,
+    token_out,
     gain_ref,
     start_ref,
     token_ref,
@@ -65,7 +69,6 @@
     kvw,
     probs,
     attended,
-    state_out,
     sel_cat,
     sel_t,
     sel_tlow,
@@ -77,7 +80,6 @@
     attended_back,
     low_part,
     high_part,
-    rows_out,
     shift,
     spread,
     query_back,
@@ -85,7 +87,6 @@
     nback,
     nback_send,
     nback_recv,
-    grad_out,
     e_src,
     e_rx1,
     e_sum,
@@ -99,11 +100,11 @@
     head_mask,
     mean_mat,
     load_sem,
-    out_sem,
     send_sem,
     recv_sem,
 ):
     A, B, planes, rows, channels, windows, heads, qw, keys, toks, width = sizes
+    state_out, grad_out = state_out_ref.at[0], grad_out_ref.at[0]
     margin = keys // 2 + qw // 2
     full = rows + 2 * margin
     span = keys + 2 * qw
@@ -140,6 +141,9 @@
         load(token_hbm.at[pl.ds(pl.multiple_of(me * tile, 8), tile)], token_ref.at[pl.ds(tile, tile)], 12),
         load(token_hbm.at[pl.ds(above, tile)], token_ref.at[pl.ds(2 * tile, tile)], 13),
     ]
+    for copy in loads[:4] + loads[9:10]:
+        copy.start()
+
     barrier = pltpu.get_barrier_semaphore()
 
     rank = lax.div(smp, Z) * A + me
@@ -166,7 +170,9 @@
     lax.fori_loop(1, G, greet, 0)
     lax.fori_loop(1, Z, greet_line, 0)
 
-    for copy in loads:
+    for copy in loads[4:9]:
+        copy.start()
+    for copy in loads[10:]:
         copy.start()
 
     def send(src, dst, index, device):
@@ -379,12 +385,6 @@
     part_down.start()
     lax.fori_loop(1, rows // block, lambda c, _: (token_part(c), 0)[1], 0)
 
-    def store(src, dst, index):
-        return pltpu.make_async_copy(src, dst, out_sem.at[index])
-
-    out_state = store(state_out, state_out_hbm.at[0], 0)
-    out_state.start()
-
     def stacked(x, y):
         return jnp.concatenate(
             [x.reshape(G // 2, half, channels), y.reshape(G // 2, half, channels)], axis=1
@@ -402,12 +402,13 @@
     e_src[second, :, pl.ds(channels, channels)] = stacked(output_high, output_sum - output_high)
 
     def scatter(src, rx, index):
-        def one(d, _):
+        def one(i, _):
+            d = 1 + lax.rem(i + G // 4, G - 1)
             peer = lax.rem(rank + d, G)
             send(src.at[peer], rx.at[d], index, plane_peer(peer)).start()
             return 0
 
-        lax.fori_loop(1, G, one, 0)
+        lax.fori_loop(0, G - 1, one, 0)
 
     def scattered(src, rx, part, rx2, index):
         wait_bytes(rx.at[pl.ds(1, G - 1)], recv_sem.at[index])
@@ -434,12 +435,12 @@
         fin[rank] = total.astype(bf16)
 
     def gather(fin, index):
-        def one(d, _):
-            peer = lax.rem(rank + d, G)
+        def one(i, _):
+            peer = lax.rem(rank + 1 + lax.rem(i + G // 4, G - 1), G)
             send(fin.at[rank], fin.at[rank], index, plane_peer(peer)).start()
             return 0
 
-        lax.fori_loop(1, G, one, 0)
+        lax.fori_loop(0, G - 1, one, 0)
 
     def gathered(fin, index):
         wait_bytes(fin.at[pl.ds(0, G - 1)], recv_sem.at[index])
@@ -485,8 +486,6 @@
         return 0
 
     lax.fori_loop(0, windows // group, backward_group, 0)
-    scattered(e_src, e_rx1, e_sum, e_rx2, 4)
-    exchange(e_sum, e_rx2, 5)
 
     own = pl.ds(margin, rows)
     spread_low[:, pl.ds(0, channels)] = spread[0].astype(bf16)
@@ -515,11 +514,9 @@
 
     part_down.wait_recv()
     own_part = nn(sel_t[...], silu[...])
-    rows_out[...] = (
+    rows_out_ref[0] = (
         (own_part + high_part[...].astype(f32)) * inv_own[:, pl.ds(0, 1)]
     ).astype(bf16)
-    out_rows = store(rows_out, rows_out_hbm.at[0], 1)
-    out_rows.start()
 
     def norm_back(r, count, extra):
         here = pl.ds(r, count)
@@ -536,6 +533,8 @@
 
     for r in range(0, rows - 2 * margin, 288):
         norm_back(margin + r, min(288, rows - 2 * margin - r), None)
+    scattered(e_src, e_rx1, e_sum, e_rx2, 4)
+    exchange(e_sum, e_rx2, 5)
     scattered(l_src, l_rx1, l_sum, l_rx2, 9)
     exchange(l_sum, l_rx2, 10)
     exchanged(e_rx2, e_fin, 5)
@@ -544,16 +543,26 @@
     back_right.wait_recv()
     norm_back(0, margin, nback_recv[0].astype(f32))
     norm_back(rows - margin, margin, nback_recv[1].astype(f32))
-    out_grad = store(grad_out, grad_out_hbm.at[0], 2)
-    out_grad.start()
     exchanged(l_rx2, l_fin, 10)
     gather(l_fin, 11)
     gathered(e_fin, 6)
-    out_early = store(e_fin, early_out_hbm, 3)
-    out_early.start()
+    scale = 1.0 / math.sqrt(B * A * rows)
+    upper, lower = slice(0, half), slice(half, 2 * half)
+
+    def matrix(ref, part, piece, column):
+        chunk = ref[part, piece, column * channels : (column + 1) * channels]
+        return chunk.astype(f32).reshape(channels, channels) * scale
+
+    for index, (part, column) in enumerate(((first, 0), (first, 1), (second, 0))):
+        for k, piece in enumerate((upper, lower)):
+            to = pl.ds((2 * index + k) * channels, channels)
+            token_out[:, to] = matrix(e_fin, part, piece, column)
+    output_out[...] = matrix(e_fin, second, upper, 1) + matrix(e_fin, second, lower, 1)
     gathered(l_fin, 11)
-    out_late = store(l_fin, late_out_hbm, 4)
-    out_late.start()
+    query_out[...] = matrix(l_fin, first, upper, 0)
+    key_out[...] = matrix(l_fin, first, lower, 0)
+    value_out[...] = matrix(l_fin, second, upper, 0)
+    gain_out[...] = jnp.sum(matrix(l_fin, second, lower, 0), axis=0, keepdims=True)
 
     for copy in (halo_left, halo_right, tokens_up, part_down, back_left, back_right):
         copy.wait_send()
@@ -566,90 +575,17 @@
         (11, l_fin, G),
     ):
         wait_bytes(ref.at[pl.ds(0, count - 1)], send_sem.at[index])
-    for copy in (out_state, out_rows, out_grad, out_early, out_late):
-        copy.wait()
-
-
-def finish(
-    scale,
-    state_hbm,
-    rows_hbm,
-    grad_hbm,
-    late_hbm,
-    early_hbm,
-    state_out,
-    rows_out,
-    grad_out,
-    gain_out,
-    query_out,
-    key_out,
-    value_out,
-    output_out,
-    token_out,
-    grad,
-    state,
-    token_rows,
-    late,
-    early,
-    gain,
-    square,
-    token,
-    in_sem,
-    out_sem,
-):
-    G, fold, _ = early.shape
-    half = fold // 2
-    channels = late.shape[2]
-    first, second = slice(0, G // 2), slice(G // 2, G)
-    upper, lower = slice(0, half), slice(half, fold)
-
-    def matrix(ref, part, piece, column):
-        chunk = ref[part, piece, column * channels : (column + 1) * channels]
-        return chunk.astype(f32).reshape(channels, channels) * scale
-
-    get_late = pltpu.make_async_copy(late_hbm, late, in_sem.at[0])
-    get_early = pltpu.make_async_copy(early_hbm, early, in_sem.at[1])
-    get_early.start()
-    get_late.start()
-    gets = [
-        pltpu.make_async_copy(src, dst, in_sem.at[2 + index])
-        for index, (src, dst) in enumerate(
-            ((grad_hbm, grad), (state_hbm, state), (rows_hbm, token_rows))
-        )
+
+
+def finish(*refs):
+    count = len(refs) // 2
+    copies = [
+        pltpu.make_async_copy(refs[index], refs[count + index], refs[-1].at[index])
+        for index in range(count)
     ]
-    for get in gets:
-        get.start()
-    puts = []
-
-    def put(src, dst, index):
-        copy = pltpu.make_async_copy(src, dst, out_sem.at[index])
+    for copy in copies:
         copy.start()
-        puts.append(copy)
-
-    for index, (src, dst) in enumerate(
-        ((grad, grad_out), (state, state_out), (token_rows, rows_out))
-    ):
-        gets[index].wait()
-        put(src, dst, index)
-    get_early.wait()
-    places = ((first, 0), (first, 1), (second, 0))
-    for index, (part, column) in enumerate(places):
-        for k, piece in enumerate((upper, lower)):
-            to = pl.ds((2 * index + k) * channels, channels)
-            token[:, to] = matrix(early, part, piece, column)
-    put(token, token_out, 3)
-    square[3] = matrix(early, second, upper, 1) + matrix(early, second, lower, 1)
-    put(square.at[3], output_out, 4)
-    get_late.wait()
-    square[0] = matrix(late, first, upper, 0)
-    square[1] = matrix(late, first, lower, 0)
-    square[2] = matrix(late, second, upper, 0)
-    put(square.at[0], query_out, 5)
-    put(square.at[1], key_out, 6)
-    put(square.at[2], value_out, 7)
-    gain[...] = jnp.sum(matrix(late, second, lower, 0), axis=0, keepdims=True)
-    put(gain, gain_out, 8)
-    for copy in puts:
+    for copy in copies:
         copy.wait()
 
 
@@ -685,17 +621,38 @@
     any_spec = pl.BlockSpec(memory_space=pltpu.HBM)
     V = pltpu.VMEM
     DMA = pltpu.SemaphoreType.DMA
+    vmem_spec = pl.BlockSpec(memory_space=pltpu.VMEM)
+    square = jax.ShapeDtypeStruct((channels, channels), f32)
+    shapes = (
+        jax.ShapeDtypeStruct((1, rows, channels), bf16),
+        jax.ShapeDtypeStruct((1, toks, width), bf16),
+        jax.ShapeDtypeStruct((1, rows, channels), f32),
+        jax.ShapeDtypeStruct((1, channels), f32),
+        square,
+        square,
+        square,
+        square,
+        jax.ShapeDtypeStruct((channels, width), f32),
+    )
+    operands = (
+        atom_state,
+        norm_gain.reshape(1, channels),
+        query_weight,
+        key_weight,
+        value_weight,
+        out_weight,
+        token_weight,
+        pair_bias.reshape(windows, heads * qw, keys),
+        key_start,
+        atom_token.reshape(-1, 128),
+        cotangent_state,
+        cotangent_tokens,
+    )
     outs = pl.pallas_call(
         functools.partial(kernel, sizes),
-        out_shape=(
-            jax.ShapeDtypeStruct((1, rows, channels), bf16),
-            jax.ShapeDtypeStruct((1, toks, width), bf16),
-            jax.ShapeDtypeStruct((1, rows, channels), f32),
-            jax.ShapeDtypeStruct((G, fold, late), bf16),
-            jax.ShapeDtypeStruct((G, fold, early), bf16),
-        ),
+        out_shape=shapes,
         in_specs=[any_spec] * 12,
-        out_specs=(any_spec,) * 5,
+        out_specs=(vmem_spec,) * 9,
         scratch_shapes=[
             V((1, channels), f32),
             pltpu.SMEM((windows,), jnp.int32),
@@ -717,7 +674,6 @@
             V((windows, keys, 2 * channels), bf16),
             V((windows, heads * qw, keys), bf16),
             V((rows, channels), bf16),
-            V((rows, channels), bf16),
             V((rows, 2 * toks), bf16),
             V((toks, rows), bf16),
             V((toks, 256), bf16),
@@ -729,7 +685,6 @@
             V((rows, 2 * channels), bf16),
             V((toks, width), bf16),
             V((toks, width), bf16),
-            V((toks, width), bf16),
             V((16, keys + 4 * qw, channels), f32),
             V((2, full, channels), f32),
             V((rows, channels), bf16),
@@ -737,7 +692,6 @@
             V((full, channels), f32),
             V((2, margin, channels), bf16),
             V((2, margin, channels), bf16),
-            V((rows, channels), f32),
             V((G, fold, early), bf16),
             V((G, fold, early), bf16),
             V((fold, early), bf16),
@@ -751,58 +705,21 @@
             V((keys, channels), bf16),
             V((2 * channels, 2 * channels), bf16),
             DMA((14,)),
-            DMA((5,)),
             DMA((12,)),
             DMA((12,)),
         ],
         compiler_params=pltpu.CompilerParams(
-            collective_id=0, has_side_effects=True, vmem_limit_bytes=62 * 1024 * 1024
+            collective_id=0, has_side_effects=True, vmem_limit_bytes=30 * 1024 * 1024
         ),
         name="atom_block",
-    )(
-        atom_state,
-        norm_gain.reshape(1, channels),
-        query_weight,
-        key_weight,
-        value_weight,
-        out_weight,
-        token_weight,
-        pair_bias.reshape(windows, heads * qw, keys),
-        key_start,
-        atom_token.reshape(-1, 128),
-        cotangent_state,
-        cotangent_tokens,
-    )
-    rescale = 1.0 / math.sqrt(B * A * rows)
-    square = jax.ShapeDtypeStruct((channels, channels), f32)
+    )(*[pltpu.with_memory_space_constraint(x, pltpu.HBM) for x in operands])
     done = pl.pallas_call(
-        functools.partial(finish, rescale),
-        out_shape=(
-            jax.ShapeDtypeStruct((1, rows, channels), bf16),
-            jax.ShapeDtypeStruct((1, toks, width), bf16),
-            jax.ShapeDtypeStruct((1, rows, channels), f32),
-            jax.ShapeDtypeStruct((1, channels), f32),
-            square,
-            square,
-            square,
-            square,
-            jax.ShapeDtypeStruct((channels, width), f32),
-        ),
-        in_specs=[any_spec] * 5,
+        finish,
+        out_shape=shapes,
+        in_specs=[vmem_spec] * 9,
         out_specs=(any_spec,) * 9,
-        scratch_shapes=[
-            V((1, rows, channels), f32),
-            V((1, rows, channels), bf16),
-            V((1, toks, width), bf16),
-            V((G, fold, late), bf16),
-            V((G, fold, early), bf16),
-            V((1, channels), f32),
-            V((4, channels, channels), f32),
-            V((channels, width), f32),
-            DMA((5,)),
-            DMA((9,)),
-        ],
-        compiler_params=pltpu.CompilerParams(vmem_limit_bytes=62 * 1024 * 1024),
+        scratch_shapes=[DMA((9,))],
+        compiler_params=pltpu.CompilerParams(vmem_limit_bytes=4 * 1024 * 1024),
         name="finish",
     )(*outs)
     return done[:3] + (done[3].reshape(channels),) + done[4:]

time: 47.1 us -> 42 us (0.89)
  Pallas kernels: 46.3 us -> 41.2 us
    pallas_call x2, Pallas kernels: 46.3 us -> 41.2 us  [the longest x1 40 us: on_device(): pl.pallas_call(functools.partial(kernel, sizes), out_shape=shapes, in_spe...]
where the time goes in v5:
time: 42 us; the launch traced here: 41.9 us
  Pallas kernels  41.2 us (98%)
  between operations  0.65 us (2%)
    pallas_call x1, Pallas kernels, on_device(): pl.pallas_call(functools.partial(kernel, sizes), out_shape=shapes, in_spe...  40 us
    pallas_call x1, Pallas kernels, on_device(): pl.pallas_call(finish, out_shape=shapes, in_specs=[vmem_spec] * 9, out_sp...  1.25 us

profile of v5, /device:TPU:1, one launch (start us, length us, event | category | flops | bytes accessed | tf_op | source)
XLA Modules:
  0.0 41.9 jit_solution(12527453271551031552)
XLA Ops:
  0.6 40.0 %atom_block.1 = (bf16[1,1024,128]{2,1,0:T(8,128)(2,1)S(1)}, bf16[1,128,768]{2,1,0:T(8,128)(2,1)S(1)}, f32[1,1024,128]{2,1,0:T(8,128)S(1)}, f32[1,128]{1,0:T(1,12...) custom-call(bf16[1,1024,128]{2,1,0:T(8,128)(2,1)} %state_hbm.1, ...), custom_call_target="tpu_custom_call" | custom-call | tf_op jit(solution)/shard_map/atom_block/pallas_call | solution.py:651
  40.6 1.2 %finish.1 = (bf16[1,1024,128]{2,1,0:T(8,128)(2,1)}, bf16[1,128,768]{2,1,0:T(8,128)(2,1)}, f32[1,1024,128]{2,1,0:T(8,128)}, f32[1,128]{1,0:T(1,128)}, f32[128,128...) custom-call(bf16[1,1024,128]{2,1,0:T(8,128)(2,1)S(1)} %get-tuple-element.27.r, ...), custom_call_target="tpu_custom_call" | custom-call | tf_op jit(solution)/shard_map/finish/pallas_call | solution.py:716

commit v6 on v5

--- a/solution.py
+++ b/solution.py
@@ -141,39 +141,42 @@
         load(token_hbm.at[pl.ds(pl.multiple_of(me * tile, 8), tile)], token_ref.at[pl.ds(tile, tile)], 12),
         load(token_hbm.at[pl.ds(above, tile)], token_ref.at[pl.ds(2 * tile, tile)], 13),
     ]
-    for copy in loads[:4] + loads[9:10]:
-        copy.start()
+    for index in (0, 9, 1, 2, 3, 11, 12, 13):
+        loads[index].start()
 
     barrier = pltpu.get_barrier_semaphore()
 
-    rank = lax.div(smp, Z) * A + me
+    plane_pos = lax.div(smp, Z)
+    rank = plane_pos * A + me
     depth = lax.rem(smp, Z)
 
-    def plane_peer(p):
-        return {"sample": lax.div(p, A) * Z + depth, "atom": lax.rem(p, A)}
+    near_line = smp - depth
+    far_line = lax.rem(near_line + Z, B)
 
     def line_peer(q):
-        return {"sample": lax.div(smp, Z) * Z + q}
-
-    def greet(d, _):
-        pl.semaphore_signal(
-            barrier, inc=1, device_id=plane_peer(lax.rem(rank + d, G)), device_id_type=MESH
-        )
+        return {"sample": near_line + q}
+
+    def greet(device):
+        pl.semaphore_signal(barrier, inc=1, device_id=device, device_id_type=MESH)
         return 0
 
-    def greet_line(d, _):
-        pl.semaphore_signal(
-            barrier, inc=1, device_id=line_peer(lax.rem(depth + d, Z)), device_id_type=MESH
-        )
-        return 0
-
-    lax.fori_loop(1, G, greet, 0)
+    def greet_near(i, _):
+        return greet({"atom": lax.rem(me + i, A)})
+
+    def greet_far(i, _):
+        return greet({"sample": far_line + depth, "atom": i})
+
+    def greet_line(i, _):
+        return greet(line_peer(lax.rem(depth + i, Z)))
+
+    greet(right)
+    greet(left)
+    lax.fori_loop(2, A - 1, greet_near, 0)
+    lax.fori_loop(0, A, greet_far, 0)
     lax.fori_loop(1, Z, greet_line, 0)
 
-    for copy in loads[4:9]:
-        copy.start()
-    for copy in loads[10:]:
-        copy.start()
+    for index in (8, 10, 4, 6, 5, 7):
+        loads[index].start()
 
     def send(src, dst, index, device):
         return pltpu.make_async_remote_copy(
@@ -212,21 +215,29 @@
     head_mask[...] = jnp.where(subs // qw == lanes // head_dim, 1.0, 0.0).astype(bf16)
 
     block = 256
-    group = 8
-
-    def project(c, _):
-        r = pl.multiple_of(c * block, block)
-        unit_rows, inv, low = norm(state[pl.ds(r, block), :])
+    group = 16
+
+    spots = [pl.ds(r, block) for r in range(0, rows, block)]
+    wides = [state[here, :] for here in spots]
+    means = [nn(x, mean_mat[pl.ds(0, channels), pl.ds(0, channels)]) for x in wides]
+    centres = [x.astype(f32) - average for x, average in zip(wides, means)]
+    spreads = [
+        nn((x * x).astype(bf16), mean_mat[pl.ds(0, channels), pl.ds(0, channels)])
+        for x in centres
+    ]
+    lows = []
+    for r, x, variance in zip(range(0, rows, block), centres, spreads):
+        inv = lax.rsqrt(variance + norm_eps)
+        unit_rows = x * inv
         unit[pl.ds(margin + r, block), :] = unit_rows
         inverse[pl.ds(r, block), :] = inv
-        normed[pl.ds(margin + r, block), :] = low
+        lows.append((unit_rows * gain_ref[...]).astype(bf16))
+        normed[pl.ds(margin + r, block), :] = lows[-1]
+    for r, low in zip(range(0, rows, block), lows):
         qkv = nn(low, w3[...]).astype(bf16)
         queries[pl.ds(r, block), :] = qkv[:, :channels]
         kvf[0, pl.ds(margin + r, block), :] = qkv[:, channels : 2 * channels].astype(f32)
         kvf[1, pl.ds(margin + r, block), :] = qkv[:, 2 * channels :].astype(f32)
-        return 0
-
-    lax.fori_loop(0, rows // block, project, 0)
 
     pl.semaphore_wait(barrier, G + Z - 2)
 
@@ -239,13 +250,13 @@
     halo_right.start()
     tokens_up.start()
 
+    for index in (11, 12, 13):
+        loads[index].wait()
     spread[...] = jnp.zeros((2, full, channels), f32)
     for slot in range(2 * group):
         shift[slot, pl.ds(0, 2 * qw), :] = jnp.zeros((2 * qw, channels), f32)
         shift[slot, pl.ds(2 * qw + keys, 2 * qw), :] = jnp.zeros((2 * qw, channels), f32)
 
-    for index in (11, 12, 13):
-        loads[index].wait()
     base = (me * toks).astype(f32)
     lower = base - toks
     sub_id = subs.astype(f32)
@@ -263,12 +274,10 @@
             count_low = count_low + hit
             sel_tlow[:, pl.ds(r * 128, 128)] = hit.astype(bf16)
         column = (spot - lower).astype(bf16).T.astype(f32)
-        sel_cat[pl.ds(r * 128, 128), pl.ds(0, 128)] = jnp.where(
-            column == lane_id, 1.0, 0.0
-        ).astype(bf16)
-        sel_cat[pl.ds(r * 128, 128), pl.ds(128, 128)] = jnp.where(
-            column == lane_id + toks, 1.0, 0.0
-        ).astype(bf16)
+        here = pl.ds(r * 128, 128)
+        sel_cat[here, pl.ds(128, 128)] = jnp.where(column == lane_id + toks, 1.0, 0.0).astype(bf16)
+        if r < 2:
+            sel_cat[here, pl.ds(0, 128)] = jnp.where(column == lane_id, 1.0, 0.0).astype(bf16)
     has_above = jnp.where(me < A - 1, 1.0, 0.0)
     for r in range(2):
         row = token_ref[pl.ds(2 * tile + r, 1), :].astype(f32)
@@ -287,6 +296,7 @@
     inverse_own = inverted(count_own)
     inverse_low = inverted(count_low)
     inv_own[...] = jnp.broadcast_to(inverse_own, (toks, 128))
+
     loads[8].wait()
     tokens_back[pl.ds(toks, toks), :] = (ctok[...].astype(f32) * inverse_own).astype(bf16)
 
@@ -353,37 +363,46 @@
 
     lax.fori_loop(inner, inner + 1, forward_group, 0)
 
-    tokens_up.wait_recv()
-    tokens_back[pl.ds(0, toks), :] = (ctok_low[...].astype(f32) * inverse_low).astype(bf16)
     for index in range(5, 8):
         loads[index].wait()
 
-    def token_part(c):
-        r = c * block if isinstance(c, int) else pl.multiple_of(c * block, block)
-        here = pl.ds(r, block)
-        out = (state[here, :].astype(f32) + nn(attended[here, :], wo[...])).astype(bf16)
-        state_out[here, :] = out
-        before = nn(out, wt[...])
-        sigma = 0.5 * jnp.tanh(0.5 * before) + 0.5
-        act = before * sigma
-        silu[here, :] = act.astype(bf16)
-        slope = sigma + act - act * sigma
-        per_atom = nn(sel_cat[here, :], tokens_back[...])
-        back = (per_atom * slope).astype(bf16)
-        active[here, :] = back
-        sback = (cots[here, :].astype(f32) + nt(back, wt[...])).astype(bf16)
-        state_back[here, :] = sback
-        aback = nt(sback, wo[...]).astype(bf16)
-        attended_back[here, pl.ds(0, channels)] = aback
-        attended_back[here, pl.ds(channels, channels)] = (
-            -aback.astype(f32) * attended[here, :].astype(f32)
-        ).astype(bf16)
-
-    token_part(0)
+    def token_columns(here, picked):
+        for column in range(0, width, 256):
+            part = pl.ds(column, 256)
+            before = nn(state_out[here, :], wt[:, part])
+            sigma = 0.5 * jnp.tanh(0.5 * before) + 0.5
+            act = before * sigma
+            silu[here, part] = act.astype(bf16)
+            slope = sigma + act - act * sigma
+            per_atom = nn(sel_cat[here, picked], tokens_back[picked, part])
+            active[here, part] = (per_atom * slope).astype(bf16)
+
+    def token_stage(r0, count):
+        spots = [pl.ds(r, block) for r in range(r0, r0 + count, block)]
+        for here in spots:
+            state_out[here, :] = (
+                state[here, :].astype(f32) + nn(attended[here, :], wo[...])
+            ).astype(bf16)
+        for here in spots[1:]:
+            token_columns(here, slice(toks, 2 * toks))
+        tokens_up.wait_recv()
+        tokens_back[pl.ds(0, toks), :] = (ctok_low[...].astype(f32) * inverse_low).astype(bf16)
+        token_columns(spots[0], slice(0, 2 * toks))
+        for here in spots:
+            state_back[here, :] = (
+                cots[here, :].astype(f32) + nt(active[here, :], wt[...])
+            ).astype(bf16)
+        for here in spots:
+            aback = nt(state_back[here, :], wo[...]).astype(bf16)
+            attended_back[here, pl.ds(0, channels)] = aback
+            attended_back[here, pl.ds(channels, channels)] = (
+                -aback.astype(f32) * attended[here, :].astype(f32)
+            ).astype(bf16)
+
+    token_stage(0, rows)
     low_part[...] = nn(sel_tlow[...], silu[pl.ds(0, 256), :]).astype(bf16)
     part_down = send(low_part, high_part, 3, left)
     part_down.start()
-    lax.fori_loop(1, rows // block, lambda c, _: (token_part(c), 0)[1], 0)
 
     def stacked(x, y):
         return jnp.concatenate(
@@ -401,14 +420,25 @@
     e_src[second, :, pl.ds(0, channels)] = stacked(pieces[4], pieces[5])
     e_src[second, :, pl.ds(channels, channels)] = stacked(output_high, output_sum - output_high)
 
+    far_first = lax.rem(plane_pos + 1, planes) * A
+    near_first = plane_pos * A
+
+    def to_plane(start_one):
+        def far(i, _):
+            atom = lax.rem(me + A // 4 + i, A)
+            start_one(far_first + atom, A + i, {"sample": far_line + depth, "atom": atom})
+            return 0
+
+        def near(i, _):
+            atom = lax.rem(me + i, A)
+            start_one(near_first + atom, i, {"atom": atom})
+            return 0
+
+        lax.fori_loop(0, A, far, 0)
+        lax.fori_loop(1, A, near, 0)
+
     def scatter(src, rx, index):
-        def one(i, _):
-            d = 1 + lax.rem(i + G // 4, G - 1)
-            peer = lax.rem(rank + d, G)
-            send(src.at[peer], rx.at[d], index, plane_peer(peer)).start()
-            return 0
-
-        lax.fori_loop(0, G - 1, one, 0)
+        to_plane(lambda peer, slot, device: send(src.at[peer], rx.at[slot], index, device).start())
 
     def scattered(src, rx, part, rx2, index):
         wait_bytes(rx.at[pl.ds(1, G - 1)], recv_sem.at[index])
@@ -435,12 +465,9 @@
         fin[rank] = total.astype(bf16)
 
     def gather(fin, index):
-        def one(i, _):
-            peer = lax.rem(rank + 1 + lax.rem(i + G // 4, G - 1), G)
-            send(fin.at[rank], fin.at[rank], index, plane_peer(peer)).start()
-            return 0
-
-        lax.fori_loop(0, G - 1, one, 0)
+        to_plane(
+            lambda peer, slot, device: send(fin.at[rank], fin.at[rank], index, device).start()
+        )
 
     def gathered(fin, index):
         wait_bytes(fin.at[pl.ds(0, G - 1)], recv_sem.at[index])
@@ -685,7 +712,7 @@
             V((rows, 2 * channels), bf16),
             V((toks, width), bf16),
             V((toks, width), bf16),
-            V((16, keys + 4 * qw, channels), f32),
+            V((32, keys + 4 * qw, channels), f32),
             V((2, full, channels), f32),
             V((rows, channels), bf16),
             V((full, 2 * channels), bf16),

time: 42 us -> 41.5 us (0.988)
  Pallas kernels: 41.2 us -> 40.7 us
    pallas_call x1, Pallas kernels: 40 us -> 39.5 us  [on_device(): pl.pallas_call(functools.partial(kernel, sizes), out_shape=shapes, in_spe...]
where the time goes in v6:
time: 41.5 us; the launch traced here: 41.4 us
  Pallas kernels  40.7 us (98%)
  between operations  0.65 us (2%)
    pallas_call x1, Pallas kernels, on_device(): pl.pallas_call(functools.partial(kernel, sizes), out_shape=shapes, in_spe...  39.5 us
    pallas_call x1, Pallas kernels, on_device(): pl.pallas_call(finish, out_shape=shapes, in_specs=[vmem_spec] * 9, out_sp...  1.25 us

profile of v6, /device:TPU:1, one launch (start us, length us, event | category | flops | bytes accessed | tf_op | source)
XLA Modules:
  0.0 41.4 jit_solution(14553128960982500538)
XLA Ops:
  0.6 39.5 %atom_block.1 = (bf16[1,1024,128]{2,1,0:T(8,128)(2,1)S(1)}, bf16[1,128,768]{2,1,0:T(8,128)(2,1)S(1)}, f32[1,1024,128]{2,1,0:T(8,128)S(1)}, f32[1,128]{1,0:T(1,12...) custom-call(bf16[1,1024,128]{2,1,0:T(8,128)(2,1)} %state_hbm.1, ...), custom_call_target="tpu_custom_call" | custom-call | tf_op jit(solution)/shard_map/atom_block/pallas_call | solution.py:678
  40.1 1.2 %finish.1 = (bf16[1,1024,128]{2,1,0:T(8,128)(2,1)}, bf16[1,128,768]{2,1,0:T(8,128)(2,1)}, f32[1,1024,128]{2,1,0:T(8,128)}, f32[1,128]{1,0:T(1,128)}, f32[128,128...) custom-call(bf16[1,1024,128]{2,1,0:T(8,128)(2,1)S(1)} %get-tuple-element.27.r, ...), custom_call_target="tpu_custom_call" | custom-call | tf_op jit(solution)/shard_map/finish/pallas_call | solution.py:743

commit v7 on v6

--- a/solution.py
+++ b/solution.py
@@ -434,8 +434,8 @@
             start_one(near_first + atom, i, {"atom": atom})
             return 0
 
-        lax.fori_loop(0, A, far, 0)
-        lax.fori_loop(1, A, near, 0)
+        lax.fori_loop(0, A, far, 0, unroll=4)
+        lax.fori_loop(1, A, near, 0, unroll=5)
 
     def scatter(src, rx, index):
         to_plane(lambda peer, slot, device: send(src.at[peer], rx.at[slot], index, device).start())
@@ -537,6 +537,8 @@
     back_right = send(nback_send.at[1], nback_recv.at[0], 8, right)
     back_left.start()
     back_right.start()
+    scattered(e_src, e_rx1, e_sum, e_rx2, 4)
+    exchange(e_sum, e_rx2, 5)
     nback[own, :] = nback[own, :] + nt(query_back[...], w3[:, :channels])
 
     part_down.wait_recv()
@@ -560,8 +562,6 @@
 
     for r in range(0, rows - 2 * margin, 288):
         norm_back(margin + r, min(288, rows - 2 * margin - r), None)
-    scattered(e_src, e_rx1, e_sum, e_rx2, 4)
-    exchange(e_sum, e_rx2, 5)
     scattered(l_src, l_rx1, l_sum, l_rx2, 9)
     exchange(l_sum, l_rx2, 10)
     exchanged(e_rx2, e_fin, 5)

time: 41.5 us -> 41.4 us (level)
  no operation moved by 1% of the time
where the time goes in v7:
time: 41.4 us; the launch traced here: 41.3 us
  Pallas kernels  40.7 us (98%)
  between operations  0.65 us (2%)
    pallas_call x1, Pallas kernels, on_device(): pl.pallas_call(functools.partial(kernel, sizes), out_shape=shapes, in_spe...  39.4 us
    pallas_call x1, Pallas kernels, on_device(): pl.pallas_call(finish, out_shape=shapes, in_specs=[vmem_spec] * 9, out_sp...  1.25 us

profile of v7, /device:TPU:1, one launch (start us, length us, event | category | flops | bytes accessed | tf_op | source)
XLA Modules:
  0.0 41.3 jit_solution(974584693130111766)
XLA Ops:
  0.6 39.4 %atom_block.1 = (bf16[1,1024,128]{2,1,0:T(8,128)(2,1)S(1)}, bf16[1,128,768]{2,1,0:T(8,128)(2,1)S(1)}, f32[1,1024,128]{2,1,0:T(8,128)S(1)}, f32[1,128]{1,0:T(1,12...) custom-call(bf16[1,1024,128]{2,1,0:T(8,128)(2,1)} %state_hbm.1, ...), custom_call_target="tpu_custom_call" | custom-call | tf_op jit(solution)/shard_map/atom_block/pallas_call | solution.py:678
  40.1 1.2 %finish.1 = (bf16[1,1024,128]{2,1,0:T(8,128)(2,1)}, bf16[1,128,768]{2,1,0:T(8,128)(2,1)}, f32[1,1024,128]{2,1,0:T(8,128)}, f32[1,128]{1,0:T(1,128)}, f32[128,128...) custom-call(bf16[1,1024,128]{2,1,0:T(8,128)(2,1)S(1)} %get-tuple-element.27.r, ...), custom_call_target="tpu_custom_call" | custom-call | tf_op jit(solution)/shard_map/finish/pallas_call | solution.py:743
